TPU v7x, 32 devices: a whole 2x2x4 slice. The times are simulated.
32 devices in a mesh: row: 4 (over z), col: 8 (over y, x, core).
Axes of the slice: x: 2, y: 2, z: 4, core: 2. Of those that a mesh axis runs over, the one named last changes fastest.
Arguments:
- emb: bfloat16 [131072, 512], P(('row', 'col')), may hold values from -6 to 6
- tiles: bfloat16 [256, 4, 256, 256], P(('row', 'col')), may hold values from -0.375 to 0.375
- msg_src: int32 [256, 4], P(('row', 'col')), may hold values from 0 to 15
- msg_dst: int32 [256, 4], P(('row', 'col')), may hold values from 0 to 16, as said below
- msg_count: int32 [256, 4], P(('row', 'col')), may hold values from 1 to 256
- weight: bfloat16 [512, 512], replicated, may hold values from -0.25 to 0.25
- docs: bfloat16 [256, 512], P('row'), may hold values from -0.059814453 to 0.099609375
- doc_labels: int32 [256, 8], replicated, may hold values from 0 to 131071
Outputs:
- hidden: bfloat16 [131072, 512], P(('row', 'col'))
- grad_docs: float32 [256, 512], P('row')
- grad_weight: float32 [512, 512], replicated
Inputs may be any that keep to these rules, and one draw needn't show every extreme that they name: For each sending device and each column of its row, the used slots (msg_dst below 16) come first and 16 marks an unused slot. In every row of devices some column receives all 4 slots used from every sender of that row.
All inputs are finite; a program needn't handle non-finite values.
Results may differ from a plain program's by a relative error of at most 0.0052.
Values may be sent and summed in bfloat16 or wider, within the bound.
A program may use at most 192 MiB of HBM per device.

v0:
```python
import jax
import jax.numpy as jnp
from jax import lax
from jax.sharding import PartitionSpec as P


def per_device(emb, tiles, msg_src, msg_dst, msg_count, weight, docs, doc_labels):
    n_col = lax.axis_size("col")
    n_row = lax.axis_size("row")
    label_dev, width = emb.shape
    blk = tiles.shape[-1]
    cap = tiles.shape[1]
    blk_dev = label_dev // blk
    labels_total = float(label_dev * n_row * n_col)
    pos_count = doc_labels.shape[1]
    own_blocks = emb.reshape(blk_dev, blk, width)
    picked = own_blocks[msg_src]
    messages = jnp.einsum(
        "pqij,pqjd->pqid", tiles, picked, preferred_element_type=jnp.float32
    ).astype(jnp.bfloat16)
    received, dst_seen, cnt_seen = (
        lax.all_to_all(messages, "col", split_axis=0, concat_axis=0, tiled=True),
        lax.all_to_all(
            msg_dst.astype(jnp.bfloat16), "col", split_axis=0, concat_axis=0, tiled=True
        ),
        lax.all_to_all(
            msg_count.astype(jnp.bfloat16), "col", split_axis=0, concat_axis=0, tiled=True
        ),
    )
    slots_all = n_col * cap
    block_ids = jnp.arange(blk_dev, dtype=jnp.float32)
    hot = (dst_seen.astype(jnp.float32).reshape(1, slots_all) == block_ids[:, None]).astype(
        jnp.float32
    )
    weighted = hot * cnt_seen.astype(jnp.float32).reshape(1, slots_all)
    total = jnp.dot(
        weighted.astype(jnp.bfloat16),
        received.reshape(slots_all, blk * width),
        preferred_element_type=jnp.float32,
    ).reshape(blk_dev, blk, width)
    total = total + float(blk) * own_blocks.astype(jnp.float32)
    denom = float(blk) + jnp.sum(weighted, axis=1)
    agg = (total / denom[:, None, None]).astype(jnp.bfloat16).reshape(label_dev, width)
    pre = jnp.dot(agg, weight, preferred_element_type=jnp.float32)
    hidden = jax.nn.silu(pre).astype(jnp.bfloat16)
    device = lax.axis_index("row") * n_col + lax.axis_index("col")
    label_ids = device * label_dev + jnp.arange(label_dev, dtype=jnp.int32)
    piece = lax.all_gather(docs, "row", axis=0, tiled=True)
    scores = jnp.einsum("nd,ld->nl", piece, hidden, preferred_element_type=jnp.float32)
    positive = doc_labels[:, 0:1] == label_ids[None, :]
    for which in range(1, pos_count):
        positive = positive | (doc_labels[:, which : which + 1] == label_ids[None, :])
    prob = jax.nn.sigmoid(scores)
    dscore = jnp.where(positive, (prob - 1.0) / float(pos_count), prob / labels_total).astype(
        jnp.bfloat16
    )
    rows_grad = jnp.dot(dscore, hidden, preferred_element_type=jnp.float32)
    dhid = jnp.einsum("nl,nd->ld", dscore, piece, preferred_element_type=jnp.float32)
    doc_grad = rows_grad
    dhid, doc_grad = (dhid, doc_grad)
    sig = jax.nn.sigmoid(pre)
    dpre = (dhid * sig * (1.0 + pre * (1.0 - sig))).astype(jnp.bfloat16)
    weight_part = jnp.einsum("la,lb->ab", agg, dpre, preferred_element_type=jnp.float32)
    grad_weight = lax.psum(weight_part, ("row", "col"))
    row_share = lax.psum_scatter(doc_grad, "row", scatter_dimension=0, tiled=True)
    grad_docs = lax.psum(row_share, "col")
    return (hidden, grad_docs, grad_weight)


def solution(mesh):
    in_specs = (
        P(("row", "col"), None),
        P(("row", "col"), None, None, None),
        P(("row", "col"), None),
        P(("row", "col"), None),
        P(("row", "col"), None),
        P(),
        P("row", None),
        P(),
    )
    out_specs = (P(("row", "col"), None), P("row", None), P())
    return jax.shard_map(
        per_device, mesh=mesh, in_specs=in_specs, out_specs=out_specs, check_vma=False
    )
```

profile of v0, /device:TPU:0, one launch (start us, length us, event | category | flops | bytes accessed | tf_op | source)
XLA Modules:
  0.0 378.9 jit_solution(3962591806349889559)
XLA Ops:
  8.0 0.7 convert_bitcast_fusion.2
  8.8 0.7 copy.23
  9.4 5.2 %all-to-all-start = ((bf16[8,1,4]{2,1,0:T(2,128)(2,1)}), bf16[8,1,4]{2,1,0:T(2,128)(2,1)S(1)}, u32[]{:S(2)}, u32[]{:S(2)}) async-start(bf16[8,1,4]{2,1,0:T(2,128)(2,1)} %copy.23), calls=%async_computation | async-start | bytes 8192 | tf_op jit(solution)/shard_map/all_to_all | solution.py:23
  14.6 0.7 convert_bitcast_fusion.1
  15.3 0.7 compare_select_fusion
  16.0 0.1 copy.25
  16.1 0.1 reshape.51
  16.2 0.7 copy.24
  16.9 7.2 %gather_fusion = bf16[32,256,512]{2,1,0:T(8,128)(2,1)} fusion(bf16[16,256,512]{2,1,0:T(8,128)(2,1)} %bitcast.62, s32[1024]{0:T(1024)S(1)} %pad_clamp_fusion), kind=kCustom, calls=%fused_computation | custom fusion | bytes 16777344 | tf_op jit(solution)/shard_map/gather | solution.py:17
  24.0 4.2 %all-to-all-start.1 = ((bf16[8,1,4]{2,1,0:T(2,128)(2,1)}), bf16[8,1,4]{2,1,0:T(2,128)(2,1)S(1)}, u32[]{:S(2)}, u32[]{:S(2)}) async-start(bf16[8,1,4]{2,1,0:T(2,128)(2,1)} %copy.24), calls=%async_computation.1 | async-start | bytes 8192 | tf_op jit(solution)/shard_map/all_to_all | solution.py:26
  28.2 8.1 %convert_bitcast_fusion = bf16[8,4,256,512]{2,3,1,0:T(8,128)(2,1)} fusion(bf16[8,4,256,512]{3,2,1,0:T(8,128)(2,1)} %bitcast.61, bf16[8,4,256,256]{3,2,1,0:T(8,128)(2,1)} %param.9), kind=kOutput, calls=%fused_computation.8 | convolution fusion | flops 2151677952 | bytes 20971520 | tf_op jit(solution)/shard_map/pqij,pqjd->pqid/dot_general | solution.py:18
  36.3 5.1 %all-to-all-start.2 = ((bf16[8,4,256,512]{2,3,1,0:T(8,128)(2,1)}), bf16[8,4,256,512]{2,3,1,0:T(8,128)(2,1)}, u32[]{:S(2)}, u32[]{:S(2)}) async-start(bf16[8,4,256,512]{2,3,1,0:T(8,128)(2,1)} %convert_bitcast_fusion), calls=%async_computation.2 | async-start | bytes 16777216 | tf_op jit(solution)/shard_map/all_to_all | solution.py:22
  41.4 0.0 reduce-scatter.2.cloned.1.call-start
  41.5 14.4 %all_gather.3 = bf16[256,512]{1,0:T(8,128)(2,1)S(1)} all-gather(bf16[64,512]{1,0:T(8,128)(2,1)S(1)} %copy-done.3), channel_id=1, replica_groups=mesh['row'=4,'col'=8] {'row'}, dimensions={0}, use_global_device_ids=true | all-gather | bytes 327680 | tf_op jit(solution)/shard_map/all_gather | solution.py:48
  56.0 0.1 reshape.47
  56.1 0.1 reshape.48
  56.2 0.1 select_reduce_fusion
  56.3 79.2 %all-to-all-done.2 = bf16[8,4,256,512]{2,3,1,0:T(8,128)(2,1)} async-done(((bf16[8,4,256,512]{2,3,1,0:T(8,128)(2,1)}), bf16[8,4,256,512]{2,3,1,0:T(8,128)(2,1)}, u32[]{:S(2)}, u32[]{:S(2)}) %all-to-all-start.2) | async-done | bytes 8388640 | tf_op jit(solution)/shard_map/all_to_all | solution.py:22
  135.5 14.6 %copy.33 = bf16[4,8,256,512]{3,1,2,0:T(8,128)(2,1)} copy(bf16[4,8,256,512]{2,3,1,0:T(8,128)(2,1)} %bitcast.36) | data formatting | bytes 16777216
  150.2 8.0 %divide_convert_fusion = bf16[16,256,512]{2,0,1:T(8,128)(2,1)S(1)} fusion(bf16[16,256,512]{2,1,0:T(8,128)(2,1)} %bitcast.63, f32[16]{0:T(128)S(1)} %broadcast_add_fusion, f32[32]{0:T(128)S(1)} %reshape.48, f32[32]{0:T(128)S(1)} %reshape.47, bf16[4,8,256,512]{3,1,2,0:T(8,128)(2,1)} %copy.33), kind=kOutput, calls=%fused_computation.7 | convolution fusion | flops 144704512 | bytes 16777536 | tf_op jit(solution)/shard_map/dot_general | solution.py:36
  158.1 2.4 copy.30
  160.5 5.7 %multiply_convert_fusion.1 = (bf16[4096,512]{1,0:T(8,128)(2,1)S(1)}, f32[4096,512]{1,0:T(8,128)}) fusion(bf16[4096,512]{1,0:T(8,128)(2,1)S(1)} %bitcast.64, bf16[512,512]{1,0:T(8,128)(2,1)S(1)} %copy-done), kind=kOutput, calls=%fused_computation.5 | convolution fusion | flops 2157969408 | bytes 17301504 | tf_op jit(solution)/shard_map/dot_general | solution.py:44
  166.2 4.5 %fusion.6 = bf16[256,4096]{0,1:T(8,128)(2,1)S(1)} fusion(bf16[4096,512]{1,0:T(8,128)(2,1)S(1)} %get-tuple-element.13, bf16[256,512]{1,0:T(8,128)(2,1)S(1)} %all_gather.3, s32[256]{0:T(256)S(1)} %bitcast.72, s32[256]{0:T(256)S(1)} %bitcast.73, s32[256]{0:T(256)S(1)} %bitcast.67, s32[256]{0:T(256)S(1)} %bitcast.68, s32[256]{0:T(256)S(1)} %bitcast.69, ...), kind=kOutput, calls=%fused_computation.14 | convolution fusion | flops 1097859072 | bytes 6578176 | tf_op jit(solution)/shard_map/nd,ld->nl/dot_general | solution.py:49
  170.7 2.1 fusion.16
  172.8 0.3 all-reduce.5.cloned.1.call-start
  173.1 10.7 %fusion.17 = f32[512,512]{1,0:T(8,128)} fusion(bf16[4096,512]{1,0:T(8,128)(2,1)} %bitcast.65, f32[4096,512]{1,0:T(8,128)} %get-tuple-element.12, bf16[256,4096]{0,1:T(8,128)(2,1)S(1)} %fusion.6, bf16[256,512]{1,0:T(8,128)(2,1)S(1)} %all_gather.3), kind=kOutput, calls=%fused_computation.33 | convolution fusion | flops 3240099840 | bytes 15990784 | tf_op jit(solution)/shard_map/la,lb->ab/dot_general | solution.py:63
  183.9 0.0 all-reduce.3.cloned.1.call-start
  183.9 10.1 %reduce-scatter.2.cloned.1.call-done = f32[64,512]{1,0:T(8,128)} async-done(((f32[256,512]{1,0:T(8,128)}), f32[64,512]{1,0:T(8,128)}) %reduce-scatter.2.cloned.1.call-update) | async-done | bytes 131088 | tf_op jit(solution)/shard_map/reduce_scatter | solution.py:65
  194.1 118.9 %all-reduce.5.cloned.1.call-done = f32[512,512]{1,0:T(8,128)} async-done(((f32[512,512]{1,0:T(8,128)}), f32[512,512]{1,0:T(8,128)}) %all-reduce.5.cloned.1.call-update) | async-done | bytes 1048592 | tf_op jit(solution)/shard_map/psum | solution.py:64
  313.0 54.6 %all-reduce.3.cloned.1.call-done = f32[64,512]{1,0:T(8,128)} async-done(((f32[64,512]{1,0:T(8,128)}), f32[64,512]{1,0:T(8,128)}) %all-reduce.3.cloned.1.call-update) | async-done | bytes 131088 | tf_op jit(solution)/shard_map/psum | solution.py:66
  367.6 1.6 copy.44
  369.2 2.3 copy.45
  (23 shorter events, 0.1 us)
Async XLA Ops:
  8.0 152.5 %copy-start = (bf16[512,512]{1,0:T(8,128)(2,1)S(1)}, bf16[512,512]{1,0:T(8,128)(2,1)}, u32[]{:S(2)}) copy-start(bf16[512,512]{1,0:T(8,128)(2,1)} %param.13) | copy-start | bytes 1572868
  9.4 14.6 %all-to-all-start = ((bf16[8,1,4]{2,1,0:T(2,128)(2,1)}), bf16[8,1,4]{2,1,0:T(2,128)(2,1)S(1)}, u32[]{:S(2)}, u32[]{:S(2)}) async-start(bf16[8,1,4]{2,1,0:T(2,128)(2,1)} %copy.23), calls=%async_computation | async-start | bytes 8192 | tf_op jit(solution)/shard_map/all_to_all | solution.py:23
  24.0 12.3 %all-to-all-start.1 = ((bf16[8,1,4]{2,1,0:T(2,128)(2,1)}), bf16[8,1,4]{2,1,0:T(2,128)(2,1)S(1)}, u32[]{:S(2)}, u32[]{:S(2)}) async-start(bf16[8,1,4]{2,1,0:T(2,128)(2,1)} %copy.24), calls=%async_computation.1 | async-start | bytes 8192 | tf_op jit(solution)/shard_map/all_to_all | solution.py:26
  36.3 5.2 %copy-start.3 = (bf16[64,512]{1,0:T(8,128)(2,1)S(1)}, bf16[64,512]{1,0:T(8,128)(2,1)}, u32[]{:S(2)}) copy-start(bf16[64,512]{1,0:T(8,128)(2,1)} %param.14) | copy-start | bytes 196612
  36.3 19.6 %copy-start.4 = (s32[256,8]{0,1:T(8,128)S(1)}, s32[256,8]{0,1:T(8,128)}, u32[]{:S(2)}) copy-start(s32[256,8]{0,1:T(8,128)} %param.15) | copy-start | bytes 24580
  36.3 99.2 %all-to-all-start.2 = ((bf16[8,4,256,512]{2,3,1,0:T(8,128)(2,1)}), bf16[8,4,256,512]{2,3,1,0:T(8,128)(2,1)}, u32[]{:S(2)}, u32[]{:S(2)}) async-start(bf16[8,4,256,512]{2,3,1,0:T(8,128)(2,1)} %convert_bitcast_fusion), calls=%async_computation.2 | async-start | bytes 16777216 | tf_op jit(solution)/shard_map/all_to_all | solution.py:22
  41.4 152.6 %reduce-scatter.2.cloned.1.call-start = ((), (), s32[]{:S(2)}) async-start(), calls=%async_computation.4 | async-start | bytes 655360 | tf_op jit(solution)/shard_map/reduce_scatter | solution.py:65
  160.5 5.7 %copy-start.2 = (bf16[16,256,512]{2,1,0:T(8,128)(2,1)}, bf16[16,256,512]{2,1,0:T(8,128)(2,1)S(1)}, u32[]{:S(2)}) copy-start(bf16[16,256,512]{2,1,0:T(8,128)(2,1)S(1)} %copy.30) | copy-start | bytes 12582916
  166.2 4.5 %copy-start.5 = (bf16[4096,512]{1,0:T(8,128)(2,1)}, bf16[4096,512]{1,0:T(8,128)(2,1)S(1)}, u32[]{:S(2)}) copy-start(bf16[4096,512]{1,0:T(8,128)(2,1)S(1)} %get-tuple-element.13) | copy-start | bytes 12582916
  172.8 140.2 %all-reduce.5.cloned.1.call-start = ((), (), s32[]{:S(2)}) async-start(), calls=%async_computation.6 | async-start | bytes 2097152 | tf_op jit(solution)/shard_map/psum | solution.py:64
  173.1 198.4 %copy-start.1 = (bf16[512,512]{1,0:T(8,128)(2,1)S(1)}, bf16[512,512]{1,0:T(8,128)(2,1)}, u32[]{:S(2)}) copy-start(bf16[512,512]{1,0:T(8,128)(2,1)} %param.13) | copy-start | bytes 1572868
  183.9 183.8 %all-reduce.3.cloned.1.call-start = ((), (), s32[]{:S(2)}) async-start(), calls=%async_computation.5 | async-start | bytes 262144 | tf_op jit(solution)/shard_map/psum | solution.py:66
Sparse Core Ops, SparseCore 0:
  173.0 21.0 reduce-scatter.1
Sparse Core Ops, SparseCore 1:
  184.0 129.0 all-reduce.4
  316.2 51.4 all-reduce.2
where the time goes:
time: 380 us; the launch traced here: 379 us
  waiting for transfers between devices  263 us (69%)
  matrix products  39 us (10%)
  local copies, waits for them, and re-layouts  29.8 us (8%)
  between operations  15.6 us (4%)
  starting transfers between devices  14.8 us (4%)
  blocking collectives  14.4 us (4%)
    psum x1, waiting for transfers between devices, per_device(): grad_weight = lax.psum(weight_part, ('row', 'col'))  119 us
    all_to_all x1, waiting for transfers between devices, per_device(): lax.all_to_all(messages, 'col', split_axis=0, concat_axis=0, tiled=True)  79.2 us
    psum x1, waiting for transfers between devices, per_device(): grad_docs = lax.psum(row_share, 'col')  54.6 us
    unnamed x15, local copies, waits for them, and re-layouts  18.5 us
    all_gather x1, blocking collectives, per_device(): piece = lax.all_gather(docs, 'row', axis=0, tiled=True)  14.4 us
    dot_general x1, matrix products, per_device(): jnp.einsum('la,lb->ab', agg, dpre, preferred_element_type=jnp.float32)  10.7 us
    reduce_scatter x1, waiting for transfers between devices, per_device(): lax.psum_scatter(doc_grad, 'row', scatter_dimension=0, tiled=True)  10.1 us
    dot_general x1, matrix products, per_device(): jnp.einsum('pqij,pqjd->pqid', tiles, picked, preferred_element_type=jnp.f...  8.08 us
  transfers between devices with their start and end apart: 6, of which 4 were waited for; matrix products, arithmetic and copies ran while one was open for 8% of the time, Pallas kernels for 0%

commit v1 on v0

v1 whole, which is shorter than its diff:
```python
import jax
import jax.numpy as jnp
from jax import lax
from jax.sharding import PartitionSpec as P


def row_pieces(blk):
    unit = blk // 8
    return ((0, 3 * unit), (3 * unit, 6 * unit), (6 * unit, blk))


def per_device(emb, tiles, msg_src, msg_dst, msg_count, weight, docs, doc_labels):
    n_col = lax.axis_size("col")
    n_row = lax.axis_size("row")
    n_dev = n_row * n_col
    row = lax.axis_index("row")
    label_dev, width = emb.shape
    blk = tiles.shape[-1]
    cap = tiles.shape[1]
    blk_dev = label_dev // blk
    labels_total = float(label_dev * n_dev)
    pos_count = doc_labels.shape[1]
    own_blocks = emb.reshape(blk_dev, blk, width)
    device = row * n_col + lax.axis_index("col")

    meta = jnp.concatenate([msg_dst, msg_count], axis=1).astype(jnp.bfloat16)
    meta = lax.all_to_all(meta, "col", split_axis=0, concat_axis=0, tiled=True)
    picked = own_blocks[msg_src]

    pieces = row_pieces(blk)
    arrived = []
    for first, last in pieces:
        message = jnp.einsum(
            "pqij,pqjd->pqid", tiles[:, :, first:last], picked, preferred_element_type=jnp.float32
        ).astype(jnp.bfloat16)
        arrived.append(lax.all_to_all(message, "col", split_axis=0, concat_axis=0, tiled=True))

    all_docs = lax.all_gather(docs, "row", axis=0, tiled=True)
    slots_all = n_col * cap
    block_ids = jnp.arange(blk_dev, dtype=jnp.float32)
    meta = meta.astype(jnp.float32)
    dst_seen = meta[:, :cap].reshape(1, slots_all)
    cnt_seen = meta[:, cap:].reshape(1, slots_all)
    weighted = jnp.where(dst_seen == block_ids[:, None], cnt_seen, 0.0)
    denom = float(blk) + jnp.sum(weighted, axis=1)
    weighted = weighted.astype(jnp.bfloat16)

    hiddens = []
    doc_part = 0.0
    weight_part = 0.0
    for (first, last), received in zip(pieces, arrived):
        rows = last - first
        count = blk_dev * rows
        total = jnp.dot(
            weighted,
            received.reshape(slots_all, rows * width),
            preferred_element_type=jnp.float32,
        ).reshape(blk_dev, rows, width)
        total = total + float(blk) * own_blocks[:, first:last].astype(jnp.float32)
        agg = (total / denom[:, None, None]).astype(jnp.bfloat16).reshape(count, width)
        pre = jnp.dot(agg, weight, preferred_element_type=jnp.float32)
        hidden = jax.nn.silu(pre).astype(jnp.bfloat16)
        label_ids = (
            device * label_dev
            + blk * jnp.arange(blk_dev, dtype=jnp.int32)[:, None]
            + jnp.arange(first, last, dtype=jnp.int32)[None, :]
        ).reshape(count)
        scores = jnp.einsum("nd,ld->nl", all_docs, hidden, preferred_element_type=jnp.float32)
        positive = doc_labels[:, 0:1] == label_ids[None, :]
        for which in range(1, pos_count):
            positive = positive | (doc_labels[:, which : which + 1] == label_ids[None, :])
        prob = jax.nn.sigmoid(scores)
        dscore = jnp.where(
            positive, (prob - 1.0) / float(pos_count), prob / labels_total
        ).astype(jnp.bfloat16)
        doc_part = doc_part + jnp.dot(dscore, hidden, preferred_element_type=jnp.float32)
        dhid = jnp.einsum("nl,nd->ld", dscore, all_docs, preferred_element_type=jnp.float32)
        sig = jax.nn.sigmoid(pre)
        dpre = (dhid * sig * (1.0 + pre * (1.0 - sig))).astype(jnp.bfloat16)
        weight_part = weight_part + jnp.einsum(
            "la,lb->ab", agg, dpre, preferred_element_type=jnp.float32
        )
        hiddens.append(hidden.reshape(blk_dev, rows, width))
    hidden = jnp.concatenate(hiddens, axis=1).reshape(label_dev, width)

    doc_rows = doc_part.shape[0] // n_dev
    weight_rows = width // n_dev
    parts = jnp.concatenate(
        [
            weight_part.astype(jnp.bfloat16).reshape(n_dev, weight_rows, width),
            doc_part.astype(jnp.bfloat16).reshape(n_dev, doc_rows, width),
        ],
        axis=1,
    )
    parts = lax.all_to_all(parts, ("row", "col"), split_axis=0, concat_axis=0, tiled=True)
    share = jnp.sum(parts.astype(jnp.float32), axis=0).astype(jnp.bfloat16)
    shares = lax.all_to_all(
        jnp.broadcast_to(share[None], (n_dev,) + share.shape),
        ("row", "col"),
        split_axis=0,
        concat_axis=0,
        tiled=True,
    )
    grad_weight = shares[:, :weight_rows].reshape(width, width).astype(jnp.float32)
    own_row = lax.dynamic_slice_in_dim(shares, row * n_col, n_col, axis=0)
    grad_docs = own_row[:, weight_rows:].reshape(n_col * doc_rows, width).astype(jnp.float32)
    return (hidden, grad_docs, grad_weight)


def solution(mesh):
    in_specs = (
        P(("row", "col"), None),
        P(("row", "col"), None, None, None),
        P(("row", "col"), None),
        P(("row", "col"), None),
        P(("row", "col"), None),
        P(),
        P("row", None),
        P(),
    )
    out_specs = (P(("row", "col"), None), P("row", None), P())
    return jax.shard_map(
        per_device, mesh=mesh, in_specs=in_specs, out_specs=out_specs, check_vma=False
    )
```

time: 380 us -> 221 us (0.58)
  waiting for transfers between devices: 263 us -> 58.9 us
  matrix products: 39 us -> 68.2 us
  blocking collectives: 14.4 us -> 39.1 us
  between operations: 15.6 us -> 0.87 us
  local copies, waits for them, and re-layouts: 29.8 us -> 20 us
  other arithmetic: 2.28 us -> 10.1 us
  starting transfers between devices: 14.8 us -> 22.2 us
    psum x2 -> x0, waiting for transfers between devices: 174 us -> none  [the longest x1 119 us: per_device(): grad_weight = lax.psum(weight_part, ('row', 'col'))]
    all_to_all x0 -> x1, blocking collectives: none -> 24.9 us  [per_device(): lax.all_to_all(parts, ('row', 'col'), split_axis=0, concat_axis=0, tiled=...]
    dot_general x4 -> x12, matrix products: 22.6 us -> 44.2 us  [the longest x3 20.7 us: per_device(): jnp.einsum('pqij,pqjd->pqid', tiles[:, :, first:last], picked, preferred_...]
    all_to_all x3 -> x5, waiting for transfers between devices: 79.2 us -> 58.9 us  [the longest x3 41.7 us: per_device(): lax.all_to_all(message, 'col', split_axis=0, concat_axis=0, tiled=True)]
    unnamed x15 -> x24, local copies, waits for them, and re-layouts: 18.5 us -> 0.94 us
    reduce_scatter x1 -> x0, waiting for transfers between devices: 10.1 us -> none  [per_device(): lax.psum_scatter(doc_grad, 'row', scatter_dimension=0, tiled=True)]
    all_to_all x3 -> x5, starting transfers between devices: 14.5 us -> 22.2 us  [the longest x3 13.3 us: per_device(): lax.all_to_all(message, 'col', split_axis=0, concat_axis=0, tiled=True)]
    slice x0 -> x4, local copies, waits for them, and re-layouts: none -> 7.41 us  [the longest x2 6.26 us: per_device(): total = total + float(blk) * own_blocks[:, first:last].astype(jnp.float32)]
  transfers between devices with their start and end apart: 6 -> 5, of which waited for: 4 -> 3; matrix products, arithmetic and copies ran while one was open for 8% -> 29% of each run, Pallas kernels for 0% -> 0%
where the time goes in v1:
time: 221 us; the launch traced here: 220 us
  matrix products  68.2 us (31%)
  waiting for transfers between devices  58.9 us (27%)
  blocking collectives  39.1 us (18%)
  starting transfers between devices  22.2 us (10%)
  local copies, waits for them, and re-layouts  20 us (9%)
  other arithmetic  10.1 us (5%)
    all_to_all x3, waiting for transfers between devices, per_device(): lax.all_to_all(message, 'col', split_axis=0, concat_axis=0, tiled=True)  41.7 us
    all_to_all x1, blocking collectives, per_device(): lax.all_to_all(parts, ('row', 'col'), split_axis=0, concat_axis=0, tiled=...  24.9 us
    dot_general x3, matrix products, per_device(): jnp.einsum('pqij,pqjd->pqid', tiles[:, :, first:last], picked, preferred_...  20.7 us
    all_to_all x1, waiting for transfers between devices, per_device(): lax.all_to_all(jnp.broadcast_to(share[None], (n_dev,) + share.shape), ('r...  17.2 us
    dot_general x3, matrix products, per_device(): jnp.einsum('la,lb->ab', agg, dpre, preferred_element_type=jnp.float32)  15.7 us
    all_gather x1, blocking collectives, per_device(): all_docs = lax.all_gather(docs, 'row', axis=0, tiled=True)  14.2 us
    dot_general x3, matrix products, per_device(): jnp.dot(weighted, received.reshape(slots_all, rows * width), preferred_el...  13.6 us
    all_to_all x3, starting transfers between devices, per_device(): lax.all_to_all(message, 'col', split_axis=0, concat_axis=0, tiled=True)  13.3 us
  transfers between devices with their start and end apart: 5, of which 3 were waited for; matrix products, arithmetic and copies ran while one was open for 29% of the time, Pallas kernels for 0%

profile of v1, /device:TPU:0, one launch (start us, length us, event | category | flops | bytes accessed | tf_op | source)
XLA Modules:
  0.0 219.6 jit_solution(14278260525141686713)
XLA Ops:
  2.1 5.2 %all-to-all-start = ((bf16[8,1,8]{2,1,0:T(2,128)(2,1)}), bf16[8,1,8]{2,1,0:T(2,128)(2,1)S(1)}, u32[]{:S(2)}, u32[]{:S(2)}) async-start(bf16[8,1,8]{2,1,0:T(2,128)(2,1)} %copy.27), calls=%async_computation | async-start | bytes 8192 | tf_op jit(solution)/shard_map/all_to_all | solution.py:27
  8.1 7.2 %gather_fusion = bf16[32,256,512]{2,1,0:T(8,128)(2,1)} fusion(bf16[16,256,512]{2,1,0:T(8,128)(2,1)} %bitcast.139, s32[1024]{0:T(1024)S(1)} %pad_clamp_fusion), kind=kCustom, calls=%fused_computation | custom fusion | bytes 16777344 | tf_op jit(solution)/shard_map/gather | solution.py:28
  15.4 6.6 %convert_bitcast_fusion.2 = bf16[8,4,64,512]{3,2,1,0:T(8,128)(2,1)} fusion(bf16[8,4,256,512]{3,2,1,0:T(8,128)(2,1)} %bitcast.136, bf16[8,4,256,256]{3,2,1,0:T(8,128)(2,1)} %param.9), kind=kOutput, calls=%fused_computation.37 | convolution fusion | flops 537919488 | bytes 11534336 | tf_op jit(solution)/shard_map/pqij,pqjd->pqid/dot_general | solution.py:33
  22.0 4.2 %all-to-all-start.3 = ((bf16[8,4,64,512]{3,2,1,0:T(8,128)(2,1)}), bf16[8,4,64,512]{3,2,1,0:T(8,128)(2,1)S(1)}, u32[]{:S(2)}, u32[]{:S(2)}) async-start(bf16[8,4,64,512]{3,2,1,0:T(8,128)(2,1)} %convert_bitcast_fusion.2), calls=%async_computation.3 | async-start | bytes 4194304 | tf_op jit(solution)/shard_map/all_to_all | solution.py:36
  26.2 2.3 %slice.92 = bf16[16,64,512]{2,1,0:T(8,128)(2,1)} slice(bf16[16,256,512]{2,1,0:T(8,128)(2,1)} %bitcast.140), slice={[0:16], [192:256], [0:512]} | slice | bytes 2097152 | tf_op jit(solution)/shard_map/slice | solution.py:59
  28.9 14.2 %all_gather.3 = bf16[256,512]{1,0:T(8,128)(2,1)S(1)} all-gather(bf16[64,512]{1,0:T(8,128)(2,1)S(1)} %copy-done.10), channel_id=1, replica_groups=mesh['row'=4,'col'=8] {'row'}, dimensions={0}, use_global_device_ids=true | all-gather | bytes 327680 | tf_op jit(solution)/shard_map/all_gather | solution.py:38
  43.2 4.0 %fusion.59 = (bf16[16,96,512]{2,1,0:T(8,128)(2,1)}, bf16[16,96,512]{2,1,0:T(8,128)(2,1)}) fusion(bf16[16,256,512]{2,1,0:T(8,128)(2,1)} %bitcast.141), kind=kLoop, calls=%fused_computation.96 | loop fusion | bytes 6291456 | tf_op jit(solution)/shard_map/slice | solution.py:59
  47.1 7.1 %convert_bitcast_fusion.1 = bf16[8,4,96,512]{3,2,1,0:T(8,128)(2,1)} fusion(bf16[8,4,256,512]{3,2,1,0:T(8,128)(2,1)} %bitcast.137, bf16[8,4,256,256]{3,2,1,0:T(8,128)(2,1)} %param.9), kind=kOutput, calls=%fused_computation.19 | convolution fusion | flops 806879232 | bytes 13107200 | tf_op jit(solution)/shard_map/pqij,pqjd->pqid/dot_general | solution.py:33
  54.2 4.5 %all-to-all-start.1 = ((bf16[8,4,96,512]{3,2,1,0:T(8,128)(2,1)}), bf16[8,4,96,512]{3,2,1,0:T(8,128)(2,1)}, u32[]{:S(2)}, u32[]{:S(2)}) async-start(bf16[8,4,96,512]{3,2,1,0:T(8,128)(2,1)} %convert_bitcast_fusion.1), calls=%async_computation.1 | async-start | bytes 6291456 | tf_op jit(solution)/shard_map/all_to_all | solution.py:36
  58.7 7.0 %convert_bitcast_fusion = bf16[8,4,96,512]{3,2,1,0:T(8,128)(2,1)} fusion(bf16[8,4,256,512]{3,2,1,0:T(8,128)(2,1)} %bitcast.138, bf16[8,4,256,256]{3,2,1,0:T(8,128)(2,1)} %param.9), kind=kOutput, calls=%fused_computation.15 | convolution fusion | flops 806879232 | bytes 13107200 | tf_op jit(solution)/shard_map/pqij,pqjd->pqid/dot_general | solution.py:33
  66.1 3.3 %divide_convert_fusion.2 = bf16[16,64,512]{2,0,1:T(8,128)(2,1)S(1)} fusion(bf16[16,64,512]{2,1,0:T(8,128)(2,1)} %slice.92, f32[16]{0:T(128)S(1)} %broadcast_add_fusion.2, f32[32]{0:T(128)S(1)} %broadcast_in_dim.18, f32[32]{0:T(128)S(1)} %eq.110, bf16[4,8,64,512]{3,2,1,0:T(8,128)(2,1)S(1)} %bitcast.146), kind=kOutput, calls=%fused_computation.36 | convolution fusion | flops 36176896 | bytes 4194624 | tf_op jit(solution)/shard_map/dot_general | solution.py:54
  69.9 2.3 %multiply_convert_fusion.3 = (bf16[1024,512]{1,0:T(8,128)(2,1)S(1)}, f32[1024,512]{1,0:T(8,128)}) fusion(bf16[1024,512]{1,0:T(8,128)(2,1)S(1)} %bitcast.151, bf16[512,512]{1,0:T(8,128)(2,1)S(1)} %copy-done), kind=kOutput, calls=%fused_computation.34 | convolution fusion | flops 539492352 | bytes 4718592 | tf_op jit(solution)/shard_map/dot_general | solution.py:61
  72.2 1.9 fusion.36
  74.1 22.4 %all-to-all-done.1 = bf16[8,4,96,512]{3,2,1,0:T(8,128)(2,1)} async-done(((bf16[8,4,96,512]{3,2,1,0:T(8,128)(2,1)}), bf16[8,4,96,512]{3,2,1,0:T(8,128)(2,1)}, u32[]{:S(2)}, u32[]{:S(2)}) %all-to-all-start.1) | async-done | bytes 3145760 | tf_op jit(solution)/shard_map/all_to_all | solution.py:36
  96.6 4.6 %all-to-all-start.2 = ((bf16[8,4,96,512]{3,2,1,0:T(8,128)(2,1)}), bf16[8,4,96,512]{3,2,1,0:T(8,128)(2,1)}, u32[]{:S(2)}, u32[]{:S(2)}) async-start(bf16[8,4,96,512]{3,2,1,0:T(8,128)(2,1)} %convert_bitcast_fusion), calls=%async_computation.2 | async-start | bytes 6291456 | tf_op jit(solution)/shard_map/all_to_all | solution.py:36
  101.2 4.9 %divide_convert_fusion.1 = bf16[16,96,512]{2,0,1:T(8,128)(2,1)S(1)} fusion(bf16[16,96,512]{2,1,0:T(8,128)(2,1)S(1)} %copy-done.5, f32[16]{0:T(128)S(1)} %broadcast_add_fusion.2, f32[32]{0:T(128)S(1)} %broadcast_in_dim.18, f32[32]{0:T(128)S(1)} %eq.110, bf16[4,8,96,512]{3,2,1,0:T(8,128)(2,1)} %bitcast.47), kind=kOutput, calls=%fused_computation.18 | convolution fusion | flops 54264832 | bytes 6291776 | tf_op jit(solution)/shard_map/dot_general | solution.py:54
  107.0 3.0 %multiply_convert_fusion.1 = (bf16[1536,512]{1,0:T(8,128)(2,1)S(1)}, f32[1536,512]{1,0:T(8,128)}) fusion(bf16[1536,512]{1,0:T(8,128)(2,1)S(1)} %bitcast.149, bf16[512,512]{1,0:T(8,128)(2,1)S(1)} %copy-done), kind=kOutput, calls=%fused_computation.16 | convolution fusion | flops 809238528 | bytes 6815744 | tf_op jit(solution)/shard_map/dot_general | solution.py:61
  110.1 1.8 fusion.26
  114.2 5.5 %fusion.35 = f32[512,512]{1,0:T(8,128)} fusion(bf16[1536,512]{1,0:T(8,128)(2,1)} %bitcast.150, f32[1536,512]{1,0:T(8,128)} %get-tuple-element.22, bf16[256,1536]{0,1:T(8,128)(2,1)} %copy-done.7, bf16[256,512]{1,0:T(8,128)(2,1)S(1)} %all_gather.3), kind=kOutput, calls=%fused_computation.55 | convolution fusion | flops 1215037440 | bytes 6815744 | tf_op jit(solution)/shard_map/la,lb->ab/dot_general | solution.py:80
  119.6 19.3 %all-to-all-done.2 = bf16[8,4,96,512]{3,2,1,0:T(8,128)(2,1)} async-done(((bf16[8,4,96,512]{3,2,1,0:T(8,128)(2,1)}), bf16[8,4,96,512]{3,2,1,0:T(8,128)(2,1)}, u32[]{:S(2)}, u32[]{:S(2)}) %all-to-all-start.2) | async-done | bytes 3145760 | tf_op jit(solution)/shard_map/all_to_all | solution.py:36
  138.9 5.4 %divide_convert_fusion = bf16[16,96,512]{2,0,1:T(8,128)(2,1)S(1)} fusion(bf16[16,96,512]{2,1,0:T(8,128)(2,1)} %get-tuple-element.4, f32[16]{0:T(128)S(1)} %broadcast_add_fusion.2, f32[32]{0:T(128)S(1)} %broadcast_in_dim.18, f32[32]{0:T(128)S(1)} %eq.110, bf16[4,8,96,512]{3,2,1,0:T(8,128)(2,1)} %bitcast.50), kind=kOutput, calls=%fused_computation.14 | convolution fusion | flops 54264832 | bytes 6291776 | tf_op jit(solution)/shard_map/dot_general | solution.py:54
  145.2 3.0 %multiply_convert_fusion = (bf16[1536,512]{1,0:T(8,128)(2,1)S(1)}, f32[1536,512]{1,0:T(8,128)}) fusion(bf16[1536,512]{1,0:T(8,128)(2,1)S(1)} %bitcast.147, bf16[512,512]{1,0:T(8,128)(2,1)S(1)} %copy-done), kind=kOutput, calls=%fused_computation.12 | convolution fusion | flops 809238528 | bytes 6815744 | tf_op jit(solution)/shard_map/dot_general | solution.py:61
  148.2 1.8 fusion.25
  150.1 1.4 convolution_add_fusion.3
  151.5 5.7 %convolution_add_fusion.1 = f32[512,512]{1,0:T(8,128)} fusion(f32[512,512]{1,0:T(8,128)} %fusion.35, bf16[1536,512]{1,0:T(8,128)(2,1)} %bitcast.148, f32[1536,512]{1,0:T(8,128)} %get-tuple-element.20, bf16[256,1536]{0,1:T(8,128)(2,1)} %copy-done.8, bf16[256,512]{1,0:T(8,128)(2,1)S(1)} %all_gather.3), kind=kOutput, calls=%fused_computation.49 | convolution fusion | flops 1215299584 | bytes 7864320 | tf_op jit(solution)/shard_map/la,lb->ab/dot_general | solution.py:80
  157.2 1.7 fusion.34
  158.9 4.5 %fusion.32 = bf16[512,512]{1,0:T(8,128)(2,1)} fusion(f32[512,512]{1,0:T(8,128)} %convolution_add_fusion.1, bf16[1024,512]{1,0:T(8,128)(2,1)} %bitcast.152, f32[1024,512]{1,0:T(8,128)} %get-tuple-element.18, bf16[256,1024]{0,1:T(8,128)(2,1)} %fusion.36, bf16[256,512]{1,0:T(8,128)(2,1)} %copy-done.9), kind=kOutput, calls=%fused_computation.50 | convolution fusion | flops 810549248 | bytes 5505024 | tf_op jit(solution)/shard_map/la,lb->ab/dot_general | solution.py:80
  164.4 24.9 %all_to_all.31 = bf16[32,24,512]{2,1,0:T(8,128)(2,1)} all-to-all(bf16[32,24,512]{2,1,0:T(8,128)(2,1)S(1)} %pad_maximum_fusion.1), channel_id=1, replica_groups=mesh['row'=4,'col'=8] {'row','col'}, dimensions={0} | all-to-all | bytes 1572864 | tf_op jit(solution)/shard_map/all_to_all | solution.py:95
  191.5 3.7 %all-to-all-start.5 = ((bf16[32,24,512]{2,1,0:T(8,128)(2,1)}), bf16[32,24,512]{2,1,0:T(8,128)(2,1)}, u32[]{:S(2)}, u32[]{:S(2)}) async-start(bf16[32,24,512]{2,1,0:T(8,128)(2,1)} %broadcast_in_dim.22), calls=%async_computation.5 | async-start | bytes 1572864 | tf_op jit(solution)/shard_map/all_to_all | solution.py:97
  195.3 3.4 %pad_maximum_fusion = bf16[16,256,512]{2,1,0:T(8,128)(2,1)} fusion(bf16[16,64,512]{2,1,0:T(8,128)(2,1)S(1)} %bitcast.145, bf16[16,96,512]{2,1,0:T(8,128)(2,1)} %bitcast.143, bf16[16,96,512]{2,1,0:T(8,128)(2,1)S(1)} %bitcast.142), kind=kLoop, calls=%fused_computation.1 | loop fusion | flops 12582912 | bytes 8388608 | tf_op jit(solution)/shard_map/concatenate | solution.py:84
  198.6 17.2 %all-to-all-done.5 = bf16[32,24,512]{2,1,0:T(8,128)(2,1)} async-done(((bf16[32,24,512]{2,1,0:T(8,128)(2,1)}), bf16[32,24,512]{2,1,0:T(8,128)(2,1)}, u32[]{:S(2)}, u32[]{:S(2)}) %all-to-all-start.5) | async-done | bytes 786464 | tf_op jit(solution)/shard_map/all_to_all | solution.py:97
  218.1 1.5 fusion.39
  (57 shorter events, 13.2 us)
Async XLA Ops:
  0.6 69.3 %copy-start = (bf16[512,512]{1,0:T(8,128)(2,1)S(1)}, bf16[512,512]{1,0:T(8,128)(2,1)}, u32[]{:S(2)}) copy-start(bf16[512,512]{1,0:T(8,128)(2,1)} %param.13) | copy-start | bytes 1572868
  2.1 19.9 %all-to-all-start = ((bf16[8,1,8]{2,1,0:T(2,128)(2,1)}), bf16[8,1,8]{2,1,0:T(2,128)(2,1)S(1)}, u32[]{:S(2)}, u32[]{:S(2)}) async-start(bf16[8,1,8]{2,1,0:T(2,128)(2,1)} %copy.27), calls=%async_computation | async-start | bytes 8192 | tf_op jit(solution)/shard_map/all_to_all | solution.py:27
  22.0 32.2 %all-to-all-start.3 = ((bf16[8,4,64,512]{3,2,1,0:T(8,128)(2,1)}), bf16[8,4,64,512]{3,2,1,0:T(8,128)(2,1)S(1)}, u32[]{:S(2)}, u32[]{:S(2)}) async-start(bf16[8,4,64,512]{3,2,1,0:T(8,128)(2,1)} %convert_bitcast_fusion.2), calls=%async_computation.3 | async-start | bytes 4194304 | tf_op jit(solution)/shard_map/all_to_all | solution.py:36
  26.2 2.7 %copy-start.10 = (bf16[64,512]{1,0:T(8,128)(2,1)S(1)}, bf16[64,512]{1,0:T(8,128)(2,1)}, u32[]{:S(2)}) copy-start(bf16[64,512]{1,0:T(8,128)(2,1)} %param.14) | copy-start | bytes 196612
  26.2 17.0 %copy-start.11 = (s32[256,8]{0,1:T(8,128)S(1)}, s32[256,8]{0,1:T(8,128)}, u32[]{:S(2)}) copy-start(s32[256,8]{0,1:T(8,128)} %param.15) | copy-start | bytes 24580
  43.1 108.3 %copy-start.9 = (bf16[256,512]{1,0:T(8,128)(2,1)}, bf16[256,512]{1,0:T(8,128)(2,1)S(1)}, u32[]{:S(2)}) copy-start(bf16[256,512]{1,0:T(8,128)(2,1)S(1)} %all_gather.3) | copy-start | bytes 786436
  54.2 42.4 %all-to-all-start.1 = ((bf16[8,4,96,512]{3,2,1,0:T(8,128)(2,1)}), bf16[8,4,96,512]{3,2,1,0:T(8,128)(2,1)}, u32[]{:S(2)}, u32[]{:S(2)}) async-start(bf16[8,4,96,512]{3,2,1,0:T(8,128)(2,1)} %convert_bitcast_fusion.1), calls=%async_computation.1 | async-start | bytes 6291456 | tf_op jit(solution)/shard_map/all_to_all | solution.py:36
  69.9 2.3 %copy-start.6 = (bf16[16,64,512]{2,1,0:T(8,128)(2,1)}, bf16[16,64,512]{2,1,0:T(8,128)(2,1)S(1)}, u32[]{:S(2)}) copy-start(bf16[16,64,512]{2,1,0:T(8,128)(2,1)S(1)} %copy.38) | copy-start | bytes 3145732
  74.1 27.1 %copy-start.5 = (bf16[16,96,512]{2,1,0:T(8,128)(2,1)S(1)}, bf16[16,96,512]{2,1,0:T(8,128)(2,1)}, u32[]{:S(2)}) copy-start(bf16[16,96,512]{2,1,0:T(8,128)(2,1)} %get-tuple-element.3) | copy-start | bytes 4718596
  96.6 42.3 %all-to-all-start.2 = ((bf16[8,4,96,512]{3,2,1,0:T(8,128)(2,1)}), bf16[8,4,96,512]{3,2,1,0:T(8,128)(2,1)}, u32[]{:S(2)}, u32[]{:S(2)}) async-start(bf16[8,4,96,512]{3,2,1,0:T(8,128)(2,1)} %convert_bitcast_fusion), calls=%async_computation.2 | async-start | bytes 6291456 | tf_op jit(solution)/shard_map/all_to_all | solution.py:36
  107.0 3.0 %copy-start.4 = (bf16[16,96,512]{2,1,0:T(8,128)(2,1)}, bf16[16,96,512]{2,1,0:T(8,128)(2,1)S(1)}, u32[]{:S(2)}) copy-start(bf16[16,96,512]{2,1,0:T(8,128)(2,1)S(1)} %copy.32) | copy-start | bytes 4718596
  111.9 0.9 copy-start.7
  145.2 3.0 %copy-start.3 = (bf16[16,96,512]{2,1,0:T(8,128)(2,1)}, bf16[16,96,512]{2,1,0:T(8,128)(2,1)S(1)}, u32[]{:S(2)}) copy-start(bf16[16,96,512]{2,1,0:T(8,128)(2,1)S(1)} %copy.35) | copy-start | bytes 4718596
  148.2 1.8 copy-start.1
  148.2 1.8 copy-start.2
  150.0 1.4 copy-start.8
  191.5 24.4 %all-to-all-start.5 = ((bf16[32,24,512]{2,1,0:T(8,128)(2,1)}), bf16[32,24,512]{2,1,0:T(8,128)(2,1)}, u32[]{:S(2)}, u32[]{:S(2)}) async-start(bf16[32,24,512]{2,1,0:T(8,128)(2,1)} %broadcast_in_dim.22), calls=%async_computation.5 | async-start | bytes 1572864 | tf_op jit(solution)/shard_map/all_to_all | solution.py:97

commit v2 on v1

--- a/solution.py
+++ b/solution.py
@@ -5,8 +5,8 @@
 
 
 def row_pieces(blk):
-    unit = blk // 8
-    return ((0, 3 * unit), (3 * unit, 6 * unit), (6 * unit, blk))
+    unit = blk // 16
+    return ((0, 8 * unit), (8 * unit, 13 * unit), (13 * unit, blk))
 
 
 def per_device(emb, tiles, msg_src, msg_dst, msg_count, weight, docs, doc_labels):
@@ -21,24 +21,28 @@
     labels_total = float(label_dev * n_dev)
     pos_count = doc_labels.shape[1]
     own_blocks = emb.reshape(blk_dev, blk, width)
-    device = row * n_col + lax.axis_index("col")
-
-    meta = jnp.concatenate([msg_dst, msg_count], axis=1).astype(jnp.bfloat16)
-    meta = lax.all_to_all(meta, "col", split_axis=0, concat_axis=0, tiled=True)
+    col = lax.axis_index("col")
+    device = row * n_col + col
     picked = own_blocks[msg_src]
 
     pieces = row_pieces(blk)
+    meta = jnp.concatenate([msg_dst, msg_count], axis=1).astype(jnp.bfloat16)
     arrived = []
     for first, last in pieces:
         message = jnp.einsum(
             "pqij,pqjd->pqid", tiles[:, :, first:last], picked, preferred_element_type=jnp.float32
         ).astype(jnp.bfloat16)
+        if arrived:
+            message, arrived[-1] = lax.optimization_barrier((message, arrived[-1]))
+        else:
+            message, docs, meta = lax.optimization_barrier((message, docs, meta))
         arrived.append(lax.all_to_all(message, "col", split_axis=0, concat_axis=0, tiled=True))
 
     all_docs = lax.all_gather(docs, "row", axis=0, tiled=True)
     slots_all = n_col * cap
     block_ids = jnp.arange(blk_dev, dtype=jnp.float32)
-    meta = meta.astype(jnp.float32)
+    meta = lax.all_gather(meta, "col", axis=0)
+    meta = lax.dynamic_index_in_dim(meta, col, axis=1, keepdims=False).astype(jnp.float32)
     dst_seen = meta[:, :cap].reshape(1, slots_all)
     cnt_seen = meta[:, cap:].reshape(1, slots_all)
     weighted = jnp.where(dst_seen == block_ids[:, None], cnt_seen, 0.0)
@@ -49,6 +53,10 @@
     doc_part = 0.0
     weight_part = 0.0
     for (first, last), received in zip(pieces, arrived):
+        if hiddens:
+            received, doc_part, weight_part = lax.optimization_barrier(
+                (received, doc_part, weight_part)
+            )
         rows = last - first
         count = blk_dev * rows
         total = jnp.dot(

time: 221 us -> 230 us (1.041)
  blocking collectives: 39.1 us -> 84.1 us
  waiting for transfers between devices: 58.9 us -> 26.6 us
  local copies, waits for them, and re-layouts: 20 us -> 27.4 us
  starting transfers between devices: 22.2 us -> 17.1 us
  matrix products: 68.2 us -> 64.5 us
    all_gather x0 -> x1, blocking collectives: none -> 44.4 us  [per_device(): meta = lax.all_gather(meta, 'col', axis=0)]
    all_to_all x3, waiting for transfers between devices: 41.7 us -> 9.43 us  [per_device(): lax.all_to_all(message, 'col', split_axis=0, concat_axis=0, tiled=True)]
    unnamed x24 -> x27, local copies, waits for them, and re-layouts: 0.94 us -> 8.61 us
    all_to_all x1 -> x0, starting transfers between devices: 5.17 us -> none  [per_device(): meta = lax.all_to_all(meta, 'col', split_axis=0, concat_axis=0, tiled=True)]
    slice x2 -> x3, local copies, waits for them, and re-layouts: 6.26 us -> 7.67 us  [per_device(): total = total + float(blk) * own_blocks[:, first:last].astype(jnp.float32)]
  transfers between devices with their start and end apart: 5 -> 4, of which waited for: 3 -> 3; matrix products, arithmetic and copies ran while one was open for 29% -> 30% of each run, Pallas kernels for 0% -> 0%
where the time goes in v2:
time: 230 us; the launch traced here: 229 us
  blocking collectives  84.1 us (37%)
  matrix products  64.5 us (28%)
  local copies, waits for them, and re-layouts  27.4 us (12%)
  waiting for transfers between devices  26.6 us (12%)
  starting transfers between devices  17.1 us (7%)
  other arithmetic  7.9 us (3%)
    all_gather x1, blocking collectives, per_device(): meta = lax.all_gather(meta, 'col', axis=0)  44.4 us
    all_to_all x1, blocking collectives, per_device(): lax.all_to_all(parts, ('row', 'col'), split_axis=0, concat_axis=0, tiled=...  24.7 us
    dot_general x3, matrix products, per_device(): jnp.einsum('pqij,pqjd->pqid', tiles[:, :, first:last], picked, preferred_...  21.7 us
    all_to_all x1, waiting for transfers between devices, per_device(): lax.all_to_all(jnp.broadcast_to(share[None], (n_dev,) + share.shape), ('r...  17.2 us
    dot_general x3, matrix products, per_device(): jnp.einsum('la,lb->ab', agg, dpre, preferred_element_type=jnp.float32)  15 us
    all_gather x1, blocking collectives, per_device(): all_docs = lax.all_gather(docs, 'row', axis=0, tiled=True)  15 us
    all_to_all x3, starting transfers between devices, per_device(): lax.all_to_all(message, 'col', split_axis=0, concat_axis=0, tiled=True)  13.5 us
    dot_general x3, matrix products, per_device(): jnp.dot(weighted, received.reshape(slots_all, rows * width), preferred_el...  11.4 us
  transfers between devices with their start and end apart: 4, of which 3 were waited for; matrix products, arithmetic and copies ran while one was open for 30% of the time, Pallas kernels for 0%

profile of v2, /device:TPU:0, one launch (start us, length us, event | category | flops | bytes accessed | tf_op | source)
XLA Modules:
  0.0 228.6 jit_solution(15765017429868252354)
XLA Ops:
  2.9 7.2 %gather_fusion = bf16[32,256,512]{2,1,0:T(8,128)(2,1)} fusion(bf16[16,256,512]{2,1,0:T(8,128)(2,1)} %bitcast.123, s32[1024]{0:T(1024)S(1)} %pad_clamp_fusion), kind=kCustom, calls=%fused_computation | custom fusion | bytes 16777344 | tf_op jit(solution)/shard_map/gather | solution.py:26
  10.1 8.4 %convert_bitcast_fusion = bf16[8,4,128,512]{2,3,1,0:T(8,128)(2,1)} fusion(bf16[8,4,256,512]{3,2,1,0:T(8,128)(2,1)} %bitcast.120, bf16[8,4,256,256]{3,2,1,0:T(8,128)(2,1)} %param.9), kind=kOutput, calls=%fused_computation.9 | convolution fusion | flops 1075838976 | bytes 14680064 | tf_op jit(solution)/shard_map/pqij,pqjd->pqid/dot_general | solution.py:32
  18.6 5.2 %all-to-all-start = ((bf16[8,4,128,512]{2,3,1,0:T(8,128)(2,1)}), bf16[8,4,128,512]{2,3,1,0:T(8,128)(2,1)}, u32[]{:S(2)}, u32[]{:S(2)}) async-start(bf16[8,4,128,512]{2,3,1,0:T(8,128)(2,1)} %convert_bitcast_fusion), calls=%async_computation | async-start | bytes 8388608 | tf_op jit(solution)/shard_map/all_to_all | solution.py:39
  23.8 2.1 slice.92
  25.8 3.1 %slice.90 = bf16[16,128,512]{2,1,0:T(8,128)(2,1)} slice(bf16[16,256,512]{2,1,0:T(8,128)(2,1)} %bitcast.125), slice={[0:16], [0:128], [0:512]} | slice | bytes 4194304 | tf_op jit(solution)/shard_map/slice | solution.py:67
  28.9 2.5 %slice.91 = bf16[16,80,512]{2,1,0:T(8,128)(2,1)} slice(bf16[16,256,512]{2,1,0:T(8,128)(2,1)} %bitcast.126), slice={[0:16], [128:208], [0:512]} | slice | bytes 2621440 | tf_op jit(solution)/shard_map/slice | solution.py:67
  31.5 44.4 %all-gather = bf16[64,8]{1,0:T(8,128)(2,1)S(1)} all-gather(bf16[8,8]{1,0:T(8,128)(2,1)S(1)} %copy.46), channel_id=2, replica_groups=mesh['row'=4,'col'=8] {'col'}, dimensions={0}, use_global_device_ids=true | all-gather | bytes 1152 | tf_op jit(solution)/shard_map/all_gather | solution.py:44
  76.6 15.0 %all_gather.11 = bf16[256,512]{1,0:T(8,128)(2,1)S(1)} all-gather(bf16[64,512]{1,0:T(8,128)(2,1)S(1)} %copy-done.10), channel_id=1, replica_groups=mesh['row'=4,'col'=8] {'row'}, dimensions={0}, use_global_device_ids=true | all-gather | bytes 327680 | tf_op jit(solution)/shard_map/all_gather | solution.py:41
  91.8 6.4 %fusion.24 = bf16[8,4,48,512]{3,2,1,0:T(8,128)(2,1)} fusion(bf16[8,4,256,512]{3,2,1,0:T(8,128)(2,1)} %bitcast.121, bf16[8,4,256,256]{3,2,1,0:T(8,128)(2,1)} %param.9), kind=kOutput, calls=%fused_computation.38 | convolution fusion | flops 403439616 | bytes 10747904 | tf_op jit(solution)/shard_map/pqij,pqjd->pqid/dot_general | solution.py:32
  98.1 6.9 %convert_bitcast_fusion.1 = bf16[8,4,80,512]{3,2,1,0:T(8,128)(2,1)} fusion(bf16[8,4,256,512]{3,2,1,0:T(8,128)(2,1)} %bitcast.122, bf16[8,4,256,256]{3,2,1,0:T(8,128)(2,1)} %param.9), kind=kOutput, calls=%fused_computation.26 | convolution fusion | flops 672399360 | bytes 12320768 | tf_op jit(solution)/shard_map/pqij,pqjd->pqid/dot_general | solution.py:32
  105.0 3.8 %all-to-all-start.1 = ((bf16[8,4,80,512]{3,2,1,0:T(8,128)(2,1)}), bf16[8,4,80,512]{3,2,1,0:T(8,128)(2,1)S(1)}, u32[]{:S(2)}, u32[]{:S(2)}) async-start(bf16[8,4,80,512]{3,2,1,0:T(8,128)(2,1)} %convert_bitcast_fusion.1), calls=%async_computation.1 | async-start | bytes 5242880 | tf_op jit(solution)/shard_map/all_to_all | solution.py:39
  108.8 7.8 %copy.69 = bf16[4,8,128,512]{3,1,2,0:T(8,128)(2,1)} copy(bf16[4,8,128,512]{2,3,1,0:T(8,128)(2,1)} %bitcast.77) | data formatting | bytes 8388608
  116.7 4.6 %divide_convert_fusion = bf16[16,128,512]{2,0,1:T(8,128)(2,1)S(1)} fusion(bf16[16,128,512]{2,1,0:T(8,128)(2,1)} %slice.90, f32[16]{0:T(128)S(1)} %broadcast_add_fusion.2, f32[32]{0:T(128)S(1)} %broadcast_in_dim.19, f32[32]{0:T(128)S(1)} %eq.126, bf16[4,8,128,512]{3,1,2,0:T(8,128)(2,1)} %copy.69), kind=kOutput, calls=%fused_computation.8 | convolution fusion | flops 72352768 | bytes 8388928 | tf_op jit(solution)/shard_map/dot_general | solution.py:62
  122.5 3.8 %multiply_convert_fusion.1 = (bf16[2048,512]{1,0:T(8,128)(2,1)S(1)}, f32[2048,512]{1,0:T(8,128)}) fusion(bf16[2048,512]{1,0:T(8,128)(2,1)S(1)} %bitcast.131, bf16[512,512]{1,0:T(8,128)(2,1)S(1)} %copy-done), kind=kOutput, calls=%fused_computation.6 | convolution fusion | flops 1078984704 | bytes 8912896 | tf_op jit(solution)/shard_map/dot_general | solution.py:69
  126.3 2.7 %select_convert_fusion = bf16[256,2048]{1,0:T(8,128)(2,1)S(1)} fusion(bf16[256,512]{1,0:T(8,128)(2,1)S(1)} %all_gather.11, bf16[2048,512]{1,0:T(8,128)(2,1)S(1)} %get-tuple-element.39, s32[2048]{0:T(1024)S(1)} %add_bitcast_fusion, s32[256]{0:T(256)S(1)} %bitcast.158, s32[256]{0:T(256)S(1)} %bitcast.161, s32[256]{0:T(256)S(1)} %bitcast.143, ...), kind=kOutput, calls=%fused_computation.28 | convolution fusion | flops 548929536 | bytes 3424256 | tf_op jit(solution)/shard_map/nd,ld->nl/dot_general | solution.py:76
  128.9 1.5 fusion.58
  130.5 6.6 %fusion.25 = f32[512,512]{1,0:T(8,128)} fusion(bf16[2048,512]{1,0:T(8,128)(2,1)} %bitcast.132, f32[2048,512]{1,0:T(8,128)} %get-tuple-element.40, bf16[256,2048]{1,0:T(8,128)(2,1)} %copy-done.12, bf16[256,512]{1,0:T(8,128)(2,1)S(1)} %all_gather.11), kind=kOutput, calls=%fused_computation.41 | convolution fusion | flops 1620049920 | bytes 8650752 | tf_op jit(solution)/shard_map/la,lb->ab/dot_general | solution.py:88
  137.0 3.8 %all-to-all-done.1 = bf16[8,4,80,512]{3,2,1,0:T(8,128)(2,1)S(1)} async-done(((bf16[8,4,80,512]{3,2,1,0:T(8,128)(2,1)}), bf16[8,4,80,512]{3,2,1,0:T(8,128)(2,1)S(1)}, u32[]{:S(2)}, u32[]{:S(2)}) %all-to-all-start.1) | async-done | bytes 2621472 | tf_op jit(solution)/shard_map/all_to_all | solution.py:39
  140.8 4.5 %all-to-all-start.2 = ((bf16[8,4,48,512]{3,2,1,0:T(8,128)(2,1)}), bf16[8,4,48,512]{3,2,1,0:T(8,128)(2,1)}, u32[]{:S(2)}, u32[]{:S(2)}) async-start(bf16[8,4,48,512]{3,2,1,0:T(8,128)(2,1)} %fusion.24), calls=%async_computation.2 | async-start | bytes 3145728 | tf_op jit(solution)/shard_map/all_to_all | solution.py:39
  145.4 3.9 %divide_convert_fusion.1 = bf16[16,80,512]{2,0,1:T(8,128)(2,1)S(1)} fusion(bf16[16,80,512]{2,1,0:T(8,128)(2,1)} %slice.91, f32[16]{0:T(128)S(1)} %broadcast_add_fusion.2, f32[32]{0:T(128)S(1)} %broadcast_in_dim.19, f32[32]{0:T(128)S(1)} %eq.126, bf16[4,8,80,512]{3,2,1,0:T(8,128)(2,1)S(1)} %bitcast.130), kind=kOutput, calls=%fused_computation.25 | convolution fusion | flops 45220864 | bytes 5243200 | tf_op jit(solution)/shard_map/dot_general | solution.py:62
  150.0 2.6 %multiply_convert_fusion.2 = (bf16[1280,512]{1,0:T(8,128)(2,1)S(1)}, f32[1280,512]{1,0:T(8,128)}) fusion(bf16[1280,512]{1,0:T(8,128)(2,1)S(1)} %bitcast.134, bf16[512,512]{1,0:T(8,128)(2,1)S(1)} %copy-done), kind=kOutput, calls=%fused_computation.23 | convolution fusion | flops 674365440 | bytes 5767168 | tf_op jit(solution)/shard_map/dot_general | solution.py:69
  152.6 1.8 select_convert_fusion.1
  155.3 5.3 %convolution_add_fusion.1 = f32[512,512]{1,0:T(8,128)} fusion(f32[512,512]{1,0:T(8,128)} %fusion.25, bf16[1280,512]{1,0:T(8,128)(2,1)} %bitcast.135, bf16[256,1280]{1,0:T(8,128)(2,1)} %copy-done.6, bf16[256,512]{1,0:T(8,128)(2,1)S(1)} %all_gather.11, f32[1280,512]{1,0:T(8,128)} %get-tuple-element.42), kind=kOutput, calls=%fused_computation.40 | convolution fusion | flops 1012793344 | bytes 6946816 | tf_op jit(solution)/shard_map/la,lb->ab/dot_general | solution.py:88
  160.6 5.6 %all-to-all-done.2 = bf16[8,4,48,512]{3,2,1,0:T(8,128)(2,1)} async-done(((bf16[8,4,48,512]{3,2,1,0:T(8,128)(2,1)}), bf16[8,4,48,512]{3,2,1,0:T(8,128)(2,1)}, u32[]{:S(2)}, u32[]{:S(2)}) %all-to-all-start.2) | async-done | bytes 1572896 | tf_op jit(solution)/shard_map/all_to_all | solution.py:39
  166.2 2.9 %divide_convert_fusion.2 = bf16[16,48,512]{2,0,1:T(8,128)(2,1)S(1)} fusion(bf16[16,48,512]{2,1,0:T(8,128)(2,1)S(1)} %copy-done.4, f32[16]{0:T(128)S(1)} %broadcast_add_fusion.2, f32[32]{0:T(128)S(1)} %broadcast_in_dim.19, f32[32]{0:T(128)S(1)} %eq.126, bf16[4,8,48,512]{3,2,1,0:T(8,128)(2,1)} %bitcast.47), kind=kOutput, calls=%fused_computation.37 | convolution fusion | flops 27132928 | bytes 3146048 | tf_op jit(solution)/shard_map/dot_general | solution.py:62
  169.6 1.8 multiply_convert_fusion.4
  171.4 1.3 select_convert_fusion.2
  173.5 3.2 %fusion.28 = bf16[512,512]{1,0:T(8,128)(2,1)S(1)} fusion(f32[512,512]{1,0:T(8,128)} %convolution_add_fusion.1, bf16[768,512]{1,0:T(8,128)(2,1)} %bitcast.137, f32[768,512]{1,0:T(8,128)} %get-tuple-element.44, bf16[256,768]{1,0:T(8,128)(2,1)} %copy-done.8, bf16[256,512]{1,0:T(8,128)(2,1)} %copy-done.9), kind=kOutput, calls=%fused_computation.46 | convolution fusion | flops 608043008 | bytes 4587520 | tf_op jit(solution)/shard_map/la,lb->ab/dot_general | solution.py:88
  176.7 24.7 %all_to_all.25 = bf16[32,24,512]{2,1,0:T(8,128)(2,1)S(1)} all-to-all(bf16[32,24,512]{2,1,0:T(8,128)(2,1)S(1)} %pad_maximum_fusion.1), channel_id=1, replica_groups=mesh['row'=4,'col'=8] {'row','col'}, dimensions={0} | all-to-all | bytes 1572864 | tf_op jit(solution)/shard_map/all_to_all | solution.py:103
  202.5 3.6 %all-to-all-start.4 = ((bf16[32,24,512]{2,1,0:T(8,128)(2,1)}), bf16[32,24,512]{2,1,0:T(8,128)(2,1)S(1)}, u32[]{:S(2)}, u32[]{:S(2)}) async-start(bf16[32,24,512]{2,1,0:T(8,128)(2,1)} %broadcast_in_dim.22), calls=%async_computation.4 | async-start | bytes 1572864 | tf_op jit(solution)/shard_map/all_to_all | solution.py:105
  206.1 3.4 %pad_maximum_fusion = bf16[16,256,512]{2,1,0:T(8,128)(2,1)} fusion(bf16[16,48,512]{2,1,0:T(8,128)(2,1)S(1)} %bitcast.129, bf16[16,80,512]{2,1,0:T(8,128)(2,1)S(1)} %bitcast.127, bf16[16,128,512]{2,1,0:T(8,128)(2,1)} %bitcast.133), kind=kLoop, calls=%fused_computation.4 | loop fusion | flops 12582912 | bytes 8388608 | tf_op jit(solution)/shard_map/concatenate | solution.py:92
  209.5 17.2 %all-to-all-done.4 = bf16[32,24,512]{2,1,0:T(8,128)(2,1)S(1)} async-done(((bf16[32,24,512]{2,1,0:T(8,128)(2,1)}), bf16[32,24,512]{2,1,0:T(8,128)(2,1)S(1)}, u32[]{:S(2)}, u32[]{:S(2)}) %all-to-all-start.4) | async-done | bytes 786464 | tf_op jit(solution)/shard_map/all_to_all | solution.py:105
  (62 shorter events, 10.1 us)
Async XLA Ops:
  0.6 121.8 %copy-start = (bf16[512,512]{1,0:T(8,128)(2,1)S(1)}, bf16[512,512]{1,0:T(8,128)(2,1)}, u32[]{:S(2)}) copy-start(bf16[512,512]{1,0:T(8,128)(2,1)} %param.13) | copy-start | bytes 1572868
  18.6 86.4 %all-to-all-start = ((bf16[8,4,128,512]{2,3,1,0:T(8,128)(2,1)}), bf16[8,4,128,512]{2,3,1,0:T(8,128)(2,1)}, u32[]{:S(2)}, u32[]{:S(2)}) async-start(bf16[8,4,128,512]{2,3,1,0:T(8,128)(2,1)} %convert_bitcast_fusion), calls=%async_computation | async-start | bytes 8388608 | tf_op jit(solution)/shard_map/all_to_all | solution.py:39
  28.9 47.6 %copy-start.10 = (bf16[64,512]{1,0:T(8,128)(2,1)S(1)}, bf16[64,512]{1,0:T(8,128)(2,1)}, u32[]{:S(2)}) copy-start(bf16[64,512]{1,0:T(8,128)(2,1)} %param.14) | copy-start | bytes 196612
  28.9 62.8 %copy-start.11 = (s32[256,8]{0,1:T(8,128)S(1)}, s32[256,8]{0,1:T(8,128)}, u32[]{:S(2)}) copy-start(s32[256,8]{0,1:T(8,128)} %param.15) | copy-start | bytes 24580
  91.5 79.9 %copy-start.9 = (bf16[256,512]{1,0:T(8,128)(2,1)}, bf16[256,512]{1,0:T(8,128)(2,1)S(1)}, u32[]{:S(2)}) copy-start(bf16[256,512]{1,0:T(8,128)(2,1)S(1)} %all_gather.11) | copy-start | bytes 786436
  105.0 35.8 %all-to-all-start.1 = ((bf16[8,4,80,512]{3,2,1,0:T(8,128)(2,1)}), bf16[8,4,80,512]{3,2,1,0:T(8,128)(2,1)S(1)}, u32[]{:S(2)}, u32[]{:S(2)}) async-start(bf16[8,4,80,512]{3,2,1,0:T(8,128)(2,1)} %convert_bitcast_fusion.1), calls=%async_computation.1 | async-start | bytes 5242880 | tf_op jit(solution)/shard_map/all_to_all | solution.py:39
  122.5 3.8 %copy-start.1 = (bf16[16,128,512]{2,1,0:T(8,128)(2,1)}, bf16[16,128,512]{2,1,0:T(8,128)(2,1)S(1)}, u32[]{:S(2)}) copy-start(bf16[16,128,512]{2,1,0:T(8,128)(2,1)S(1)} %copy.52) | copy-start | bytes 6291460
  126.3 2.7 %copy-start.2 = (bf16[2048,512]{1,0:T(8,128)(2,1)}, bf16[2048,512]{1,0:T(8,128)(2,1)S(1)}, u32[]{:S(2)}) copy-start(bf16[2048,512]{1,0:T(8,128)(2,1)S(1)} %get-tuple-element.39) | copy-start | bytes 6291460
  128.9 1.5 copy-start.12
  140.8 25.3 %all-to-all-start.2 = ((bf16[8,4,48,512]{3,2,1,0:T(8,128)(2,1)}), bf16[8,4,48,512]{3,2,1,0:T(8,128)(2,1)}, u32[]{:S(2)}, u32[]{:S(2)}) async-start(bf16[8,4,48,512]{3,2,1,0:T(8,128)(2,1)} %fusion.24), calls=%async_computation.2 | async-start | bytes 3145728 | tf_op jit(solution)/shard_map/all_to_all | solution.py:39
  150.0 2.6 %copy-start.3 = (bf16[16,80,512]{2,1,0:T(8,128)(2,1)}, bf16[16,80,512]{2,1,0:T(8,128)(2,1)S(1)}, u32[]{:S(2)}) copy-start(bf16[16,80,512]{2,1,0:T(8,128)(2,1)S(1)} %copy.55) | copy-start | bytes 3932164
  152.6 1.8 copy-start.7
  154.4 0.9 copy-start.6
  155.3 10.9 %copy-start.4 = (bf16[16,48,512]{2,1,0:T(8,128)(2,1)S(1)}, bf16[16,48,512]{2,1,0:T(8,128)(2,1)}, u32[]{:S(2)}) copy-start(bf16[16,48,512]{2,1,0:T(8,128)(2,1)} %slice.92) | copy-start | bytes 2359300
  169.6 1.9 copy-start.5
  172.8 0.7 copy-start.8
  202.5 24.2 %all-to-all-start.4 = ((bf16[32,24,512]{2,1,0:T(8,128)(2,1)}), bf16[32,24,512]{2,1,0:T(8,128)(2,1)S(1)}, u32[]{:S(2)}, u32[]{:S(2)}) async-start(bf16[32,24,512]{2,1,0:T(8,128)(2,1)} %broadcast_in_dim.22), calls=%async_computation.4 | async-start | bytes 1572864 | tf_op jit(solution)/shard_map/all_to_all | solution.py:105

commit v3 on v2

--- a/solution.py
+++ b/solution.py
@@ -6,7 +6,7 @@
 
 def row_pieces(blk):
     unit = blk // 16
-    return ((0, 8 * unit), (8 * unit, 13 * unit), (13 * unit, blk))
+    return ((0, 7 * unit), (7 * unit, 13 * unit), (13 * unit, blk))
 
 
 def per_device(emb, tiles, msg_src, msg_dst, msg_count, weight, docs, doc_labels):
@@ -21,12 +21,12 @@
     labels_total = float(label_dev * n_dev)
     pos_count = doc_labels.shape[1]
     own_blocks = emb.reshape(blk_dev, blk, width)
-    col = lax.axis_index("col")
-    device = row * n_col + col
+    device = row * n_col + lax.axis_index("col")
     picked = own_blocks[msg_src]
 
     pieces = row_pieces(blk)
     meta = jnp.concatenate([msg_dst, msg_count], axis=1).astype(jnp.bfloat16)
+    meta = lax.all_to_all(meta, "col", split_axis=0, concat_axis=0, tiled=True)
     arrived = []
     for first, last in pieces:
         message = jnp.einsum(
@@ -41,8 +41,7 @@
     all_docs = lax.all_gather(docs, "row", axis=0, tiled=True)
     slots_all = n_col * cap
     block_ids = jnp.arange(blk_dev, dtype=jnp.float32)
-    meta = lax.all_gather(meta, "col", axis=0)
-    meta = lax.dynamic_index_in_dim(meta, col, axis=1, keepdims=False).astype(jnp.float32)
+    meta = meta.astype(jnp.float32)
     dst_seen = meta[:, :cap].reshape(1, slots_all)
     cnt_seen = meta[:, cap:].reshape(1, slots_all)
     weighted = jnp.where(dst_seen == block_ids[:, None], cnt_seen, 0.0)

time: 230 us -> 206 us (0.90)
  blocking collectives: 84.1 us -> 38.7 us
  waiting for transfers between devices: 26.6 us -> 45.7 us
  local copies, waits for them, and re-layouts: 27.4 us -> 20.7 us
  starting transfers between devices: 17.1 us -> 22.6 us
    all_gather x1 -> x0, blocking collectives: 44.4 us -> none  [per_device(): meta = lax.all_gather(meta, 'col', axis=0)]
    all_to_all x3, waiting for transfers between devices: 9.43 us -> 28.5 us  [per_device(): lax.all_to_all(message, 'col', split_axis=0, concat_axis=0, tiled=True)]
    unnamed x27, local copies, waits for them, and re-layouts: 8.61 us -> 1.39 us
    all_to_all x0 -> x1, starting transfers between devices: none -> 5.17 us  [per_device(): meta = lax.all_to_all(meta, 'col', split_axis=0, concat_axis=0, tiled=True)]
    dot_general x3, matrix products: 11.4 us -> 13.9 us  [per_device(): jnp.dot(weighted, received.reshape(slots_all, rows * width), preferred_el...]
  transfers between devices with their start and end apart: 4 -> 5, of which waited for: 3 -> 4; matrix products, arithmetic and copies ran while one was open for 30% -> 37% of each run, Pallas kernels for 0% -> 0%
where the time goes in v3:
time: 206 us; the launch traced here: 205 us
  matrix products  66.7 us (32%)
  waiting for transfers between devices  45.7 us (22%)
  blocking collectives  38.7 us (19%)
  starting transfers between devices  22.6 us (11%)
  local copies, waits for them, and re-layouts  20.7 us (10%)
  other arithmetic  10.1 us (5%)
    all_to_all x3, waiting for transfers between devices, per_device(): lax.all_to_all(message, 'col', split_axis=0, concat_axis=0, tiled=True)  28.5 us
    all_to_all x1, blocking collectives, per_device(): lax.all_to_all(parts, ('row', 'col'), split_axis=0, concat_axis=0, tiled=...  24.6 us
    dot_general x3, matrix products, per_device(): jnp.einsum('pqij,pqjd->pqid', tiles[:, :, first:last], picked, preferred_...  20.6 us
    all_to_all x1, waiting for transfers between devices, per_device(): lax.all_to_all(jnp.broadcast_to(share[None], (n_dev,) + share.shape), ('r...  17.3 us
    dot_general x3, matrix products, per_device(): jnp.einsum('la,lb->ab', agg, dpre, preferred_element_type=jnp.float32)  15.9 us
    all_gather x1, blocking collectives, per_device(): all_docs = lax.all_gather(docs, 'row', axis=0, tiled=True)  14.1 us
    dot_general x3, matrix products, per_device(): jnp.dot(weighted, received.reshape(slots_all, rows * width), preferred_el...  13.9 us
    all_to_all x3, starting transfers between devices, per_device(): lax.all_to_all(message, 'col', split_axis=0, concat_axis=0, tiled=True)  13.7 us
  transfers between devices with their start and end apart: 5, of which 4 were waited for; matrix products, arithmetic and copies ran while one was open for 37% of the time, Pallas kernels for 0%

profile of v3, /device:TPU:0, one launch (start us, length us, event | category | flops | bytes accessed | tf_op | source)
XLA Modules:
  0.0 205.4 jit_solution(2162860878747446817)
XLA Ops:
  2.1 5.2 %all-to-all-start = ((bf16[8,1,8]{2,1,0:T(2,128)(2,1)}), bf16[8,1,8]{2,1,0:T(2,128)(2,1)S(1)}, u32[]{:S(2)}, u32[]{:S(2)}) async-start(bf16[8,1,8]{2,1,0:T(2,128)(2,1)} %copy.39), calls=%async_computation | async-start | bytes 8192 | tf_op jit(solution)/shard_map/all_to_all | solution.py:29
  8.1 7.2 %gather_fusion = bf16[32,256,512]{2,1,0:T(8,128)(2,1)} fusion(bf16[16,256,512]{2,1,0:T(8,128)(2,1)} %bitcast.121, s32[1024]{0:T(1024)S(1)} %pad_clamp_fusion), kind=kCustom, calls=%fused_computation | custom fusion | bytes 16777344 | tf_op jit(solution)/shard_map/gather | solution.py:25
  15.3 7.1 %convert_bitcast_fusion = bf16[8,4,112,512]{3,2,1,0:T(8,128)(2,1)} fusion(bf16[8,4,256,512]{3,2,1,0:T(8,128)(2,1)} %bitcast.118, bf16[8,4,256,256]{3,2,1,0:T(8,128)(2,1)} %param.9), kind=kOutput, calls=%fused_computation.9 | convolution fusion | flops 941359104 | bytes 13893632 | tf_op jit(solution)/shard_map/pqij,pqjd->pqid/dot_general | solution.py:32
  22.5 4.5 %all-to-all-start.1 = ((bf16[8,4,112,512]{3,2,1,0:T(8,128)(2,1)}), bf16[8,4,112,512]{3,2,1,0:T(8,128)(2,1)}, u32[]{:S(2)}, u32[]{:S(2)}) async-start(bf16[8,4,112,512]{3,2,1,0:T(8,128)(2,1)} %convert_bitcast_fusion), calls=%async_computation.1 | async-start | bytes 7340032 | tf_op jit(solution)/shard_map/all_to_all | solution.py:39
  27.0 2.1 %slice.92 = bf16[16,48,512]{2,1,0:T(8,128)(2,1)} slice(bf16[16,256,512]{2,1,0:T(8,128)(2,1)} %bitcast.122), slice={[0:16], [208:256], [0:512]} | slice | bytes 1572864 | tf_op jit(solution)/shard_map/slice | solution.py:66
  29.1 1.6 slice.90
  30.8 2.7 %slice.91 = bf16[16,96,512]{2,1,0:T(8,128)(2,1)} slice(bf16[16,256,512]{2,1,0:T(8,128)(2,1)} %bitcast.124), slice={[0:16], [112:208], [0:512]} | slice | bytes 3145728 | tf_op jit(solution)/shard_map/slice | solution.py:66
  34.0 6.4 %fusion.25 = bf16[8,4,48,512]{3,2,1,0:T(8,128)(2,1)} fusion(bf16[8,4,256,512]{3,2,1,0:T(8,128)(2,1)} %bitcast.119, bf16[8,4,256,256]{3,2,1,0:T(8,128)(2,1)} %param.9), kind=kOutput, calls=%fused_computation.40 | convolution fusion | flops 403439616 | bytes 10747904 | tf_op jit(solution)/shard_map/pqij,pqjd->pqid/dot_general | solution.py:32
  40.3 7.0 %convert_bitcast_fusion.1 = bf16[8,4,96,512]{3,2,1,0:T(8,128)(2,1)} fusion(bf16[8,4,256,512]{3,2,1,0:T(8,128)(2,1)} %bitcast.120, bf16[8,4,256,256]{3,2,1,0:T(8,128)(2,1)} %param.9), kind=kOutput, calls=%fused_computation.18 | convolution fusion | flops 806879232 | bytes 13107200 | tf_op jit(solution)/shard_map/pqij,pqjd->pqid/dot_general | solution.py:32
  47.6 14.1 %all_gather.3 = bf16[256,512]{1,0:T(8,128)(2,1)S(1)} all-gather(bf16[64,512]{1,0:T(8,128)(2,1)S(1)} %copy-done.11), channel_id=1, replica_groups=mesh['row'=4,'col'=8] {'row'}, dimensions={0}, use_global_device_ids=true | all-gather | bytes 327680 | tf_op jit(solution)/shard_map/all_gather | solution.py:41
  61.9 8.7 %all-to-all-done.1 = bf16[8,4,112,512]{3,2,1,0:T(8,128)(2,1)} async-done(((bf16[8,4,112,512]{3,2,1,0:T(8,128)(2,1)}), bf16[8,4,112,512]{3,2,1,0:T(8,128)(2,1)}, u32[]{:S(2)}, u32[]{:S(2)}) %all-to-all-start.1) | async-done | bytes 3670048 | tf_op jit(solution)/shard_map/all_to_all | solution.py:39
  70.5 4.6 %all-to-all-start.2 = ((bf16[8,4,96,512]{3,2,1,0:T(8,128)(2,1)}), bf16[8,4,96,512]{3,2,1,0:T(8,128)(2,1)}, u32[]{:S(2)}, u32[]{:S(2)}) async-start(bf16[8,4,96,512]{3,2,1,0:T(8,128)(2,1)} %convert_bitcast_fusion.1), calls=%async_computation.2 | async-start | bytes 6291456 | tf_op jit(solution)/shard_map/all_to_all | solution.py:39
  75.2 5.6 %divide_convert_fusion = bf16[16,112,512]{2,0,1:T(8,128)(2,1)S(1)} fusion(bf16[16,112,512]{2,1,0:T(8,128)(2,1)S(1)} %slice.90, f32[16]{0:T(128)S(1)} %broadcast_add_fusion.2, f32[32]{0:T(128)S(1)} %broadcast_in_dim.19, f32[32]{0:T(128)S(1)} %eq.126, bf16[4,8,112,512]{3,2,1,0:T(8,128)(2,1)} %bitcast.40), kind=kOutput, calls=%fused_computation.8 | convolution fusion | flops 63308800 | bytes 7340352 | tf_op jit(solution)/shard_map/dot_general | solution.py:61
  81.8 3.4 %multiply_convert_fusion.1 = (bf16[1792,512]{1,0:T(8,128)(2,1)S(1)}, f32[1792,512]{1,0:T(8,128)}) fusion(bf16[1792,512]{1,0:T(8,128)(2,1)S(1)} %bitcast.129, bf16[512,512]{1,0:T(8,128)(2,1)S(1)} %copy-done), kind=kOutput, calls=%fused_computation.6 | convolution fusion | flops 944111616 | bytes 7864320 | tf_op jit(solution)/shard_map/dot_general | solution.py:68
  85.2 2.3 %select_convert_fusion = bf16[256,1792]{1,0:T(8,128)(2,1)S(1)} fusion(bf16[256,512]{1,0:T(8,128)(2,1)S(1)} %all_gather.3, bf16[1792,512]{1,0:T(8,128)(2,1)S(1)} %get-tuple-element.39, s32[1792]{0:T(1024)S(1)} %add.182, s32[256]{0:T(256)S(1)} %bitcast.155, s32[256]{0:T(256)S(1)} %bitcast.158, s32[256]{0:T(256)S(1)} %bitcast.140, s32[256]{0:T(256)S(1)} %bitcast.143, ...), kind=kOutput, calls=%fused_computation.28 | convolution fusion | flops 480313344 | bytes 3030016 | tf_op jit(solution)/shard_map/nd,ld->nl/dot_general | solution.py:75
  89.1 6.1 %fusion.30 = f32[512,512]{1,0:T(8,128)} fusion(bf16[1792,512]{1,0:T(8,128)(2,1)} %bitcast.130, f32[1792,512]{1,0:T(8,128)} %get-tuple-element.40, bf16[256,1792]{1,0:T(8,128)(2,1)} %copy-done.5, bf16[256,512]{1,0:T(8,128)(2,1)S(1)} %all_gather.3), kind=kOutput, calls=%fused_computation.48 | convolution fusion | flops 1417543680 | bytes 7733248 | tf_op jit(solution)/shard_map/la,lb->ab/dot_general | solution.py:87
  95.2 17.6 %all-to-all-done.2 = bf16[8,4,96,512]{3,2,1,0:T(8,128)(2,1)} async-done(((bf16[8,4,96,512]{3,2,1,0:T(8,128)(2,1)}), bf16[8,4,96,512]{3,2,1,0:T(8,128)(2,1)}, u32[]{:S(2)}, u32[]{:S(2)}) %all-to-all-start.2) | async-done | bytes 3145760 | tf_op jit(solution)/shard_map/all_to_all | solution.py:39
  112.9 4.5 %all-to-all-start.3 = ((bf16[8,4,48,512]{3,2,1,0:T(8,128)(2,1)}), bf16[8,4,48,512]{3,2,1,0:T(8,128)(2,1)}, u32[]{:S(2)}, u32[]{:S(2)}) async-start(bf16[8,4,48,512]{3,2,1,0:T(8,128)(2,1)} %fusion.25), calls=%async_computation.3 | async-start | bytes 3145728 | tf_op jit(solution)/shard_map/all_to_all | solution.py:39
  117.4 5.4 %divide_convert_fusion.1 = bf16[16,96,512]{2,0,1:T(8,128)(2,1)S(1)} fusion(bf16[16,96,512]{2,1,0:T(8,128)(2,1)} %slice.91, f32[16]{0:T(128)S(1)} %broadcast_add_fusion.2, f32[32]{0:T(128)S(1)} %broadcast_in_dim.19, f32[32]{0:T(128)S(1)} %eq.126, bf16[4,8,96,512]{3,2,1,0:T(8,128)(2,1)} %bitcast.43), kind=kOutput, calls=%fused_computation.17 | convolution fusion | flops 54264832 | bytes 6291776 | tf_op jit(solution)/shard_map/dot_general | solution.py:61
  123.7 3.0 %multiply_convert_fusion.2 = (bf16[1536,512]{1,0:T(8,128)(2,1)S(1)}, f32[1536,512]{1,0:T(8,128)}) fusion(bf16[1536,512]{1,0:T(8,128)(2,1)S(1)} %bitcast.131, bf16[512,512]{1,0:T(8,128)(2,1)S(1)} %copy-done), kind=kOutput, calls=%fused_computation.15 | convolution fusion | flops 809238528 | bytes 6815744 | tf_op jit(solution)/shard_map/dot_general | solution.py:68
  126.7 2.1 %select_convert_fusion.1 = bf16[256,1536]{1,0:T(8,128)(2,1)S(1)} fusion(bf16[256,512]{1,0:T(8,128)(2,1)S(1)} %all_gather.3, bf16[1536,512]{1,0:T(8,128)(2,1)S(1)} %get-tuple-element.41, s32[1536]{0:T(1024)S(1)} %add.192, s32[256]{0:T(256)S(1)} %bitcast.156, s32[256]{0:T(256)S(1)} %bitcast.159, s32[256]{0:T(256)S(1)} %bitcast.141, s32[256]{0:T(256)S(1)} %bitcast.144, ...), kind=kOutput, calls=%fused_computation.38 | convolution fusion | flops 411697152 | bytes 2635776 | tf_op jit(solution)/shard_map/nd,ld->nl/dot_general | solution.py:75
  128.9 1.4 convolution_add_fusion.3
  130.3 5.8 %convolution_add_fusion.1 = f32[512,512]{1,0:T(8,128)} fusion(f32[512,512]{1,0:T(8,128)} %fusion.30, bf16[1536,512]{1,0:T(8,128)(2,1)} %bitcast.132, f32[1536,512]{1,0:T(8,128)} %get-tuple-element.42, bf16[256,1536]{1,0:T(8,128)(2,1)} %copy-done.8, bf16[256,512]{1,0:T(8,128)(2,1)S(1)} %all_gather.3), kind=kOutput, calls=%fused_computation.42 | convolution fusion | flops 1215299584 | bytes 7864320 | tf_op jit(solution)/shard_map/la,lb->ab/dot_general | solution.py:87
  136.1 2.1 %all-to-all-done.3 = bf16[8,4,48,512]{3,2,1,0:T(8,128)(2,1)} async-done(((bf16[8,4,48,512]{3,2,1,0:T(8,128)(2,1)}), bf16[8,4,48,512]{3,2,1,0:T(8,128)(2,1)}, u32[]{:S(2)}, u32[]{:S(2)}) %all-to-all-start.3) | async-done | bytes 1572896 | tf_op jit(solution)/shard_map/all_to_all | solution.py:39
  138.2 2.9 %divide_convert_fusion.2 = bf16[16,48,512]{2,0,1:T(8,128)(2,1)S(1)} fusion(bf16[16,48,512]{2,1,0:T(8,128)(2,1)S(1)} %copy-done.6, f32[16]{0:T(128)S(1)} %broadcast_add_fusion.2, f32[32]{0:T(128)S(1)} %broadcast_in_dim.19, f32[32]{0:T(128)S(1)} %eq.126, bf16[4,8,48,512]{3,2,1,0:T(8,128)(2,1)} %bitcast.46), kind=kOutput, calls=%fused_computation.37 | convolution fusion | flops 27132928 | bytes 3146048 | tf_op jit(solution)/shard_map/dot_general | solution.py:61
  141.6 1.8 multiply_convert_fusion.4
  145.6 4.0 %fusion.27 = bf16[512,512]{1,0:T(8,128)(2,1)} fusion(f32[512,512]{1,0:T(8,128)} %convolution_add_fusion.1, bf16[768,512]{1,0:T(8,128)(2,1)} %bitcast.134, f32[768,512]{1,0:T(8,128)} %get-tuple-element.44, bf16[256,768]{1,0:T(8,128)(2,1)} %copy-done.9, bf16[256,512]{1,0:T(8,128)(2,1)} %copy-done.10), kind=kOutput, calls=%fused_computation.45 | convolution fusion | flops 608043008 | bytes 4587520 | tf_op jit(solution)/shard_map/la,lb->ab/dot_general | solution.py:87
  150.6 24.6 %all_to_all.34 = bf16[32,24,512]{2,1,0:T(8,128)(2,1)} all-to-all(bf16[32,24,512]{2,1,0:T(8,128)(2,1)S(1)} %pad_maximum_fusion.1), channel_id=1, replica_groups=mesh['row'=4,'col'=8] {'row','col'}, dimensions={0} | all-to-all | bytes 1572864 | tf_op jit(solution)/shard_map/all_to_all | solution.py:102
  177.4 3.7 %all-to-all-start.5 = ((bf16[32,24,512]{2,1,0:T(8,128)(2,1)}), bf16[32,24,512]{2,1,0:T(8,128)(2,1)}, u32[]{:S(2)}, u32[]{:S(2)}) async-start(bf16[32,24,512]{2,1,0:T(8,128)(2,1)} %broadcast_in_dim.22), calls=%async_computation.5 | async-start | bytes 1572864 | tf_op jit(solution)/shard_map/all_to_all | solution.py:104
  181.1 3.3 %pad_maximum_fusion = bf16[16,256,512]{2,1,0:T(8,128)(2,1)} fusion(bf16[16,48,512]{2,1,0:T(8,128)(2,1)S(1)} %bitcast.128, bf16[16,96,512]{2,1,0:T(8,128)(2,1)} %bitcast.126, bf16[16,112,512]{2,1,0:T(8,128)(2,1)S(1)} %bitcast.125), kind=kLoop, calls=%fused_computation.1 | loop fusion | flops 12582912 | bytes 8388608 | tf_op jit(solution)/shard_map/concatenate | solution.py:91
  184.4 17.3 %all-to-all-done.5 = bf16[32,24,512]{2,1,0:T(8,128)(2,1)} async-done(((bf16[32,24,512]{2,1,0:T(8,128)(2,1)}), bf16[32,24,512]{2,1,0:T(8,128)(2,1)}, u32[]{:S(2)}, u32[]{:S(2)}) %all-to-all-start.5) | async-done | bytes 786464 | tf_op jit(solution)/shard_map/all_to_all | solution.py:104
  203.9 1.5 fusion.35
  (61 shorter events, 14.6 us)
Async XLA Ops:
  0.6 81.2 %copy-start = (bf16[512,512]{1,0:T(8,128)(2,1)S(1)}, bf16[512,512]{1,0:T(8,128)(2,1)}, u32[]{:S(2)}) copy-start(bf16[512,512]{1,0:T(8,128)(2,1)} %param.13) | copy-start | bytes 1572868
  2.1 20.4 %all-to-all-start = ((bf16[8,1,8]{2,1,0:T(2,128)(2,1)}), bf16[8,1,8]{2,1,0:T(2,128)(2,1)S(1)}, u32[]{:S(2)}, u32[]{:S(2)}) async-start(bf16[8,1,8]{2,1,0:T(2,128)(2,1)} %copy.39), calls=%async_computation | async-start | bytes 8192 | tf_op jit(solution)/shard_map/all_to_all | solution.py:29
  22.5 48.1 %all-to-all-start.1 = ((bf16[8,4,112,512]{3,2,1,0:T(8,128)(2,1)}), bf16[8,4,112,512]{3,2,1,0:T(8,128)(2,1)}, u32[]{:S(2)}, u32[]{:S(2)}) async-start(bf16[8,4,112,512]{3,2,1,0:T(8,128)(2,1)} %convert_bitcast_fusion), calls=%async_computation.1 | async-start | bytes 7340032 | tf_op jit(solution)/shard_map/all_to_all | solution.py:39
  30.7 3.2 %copy-start.12 = (s32[256,8]{0,1:T(8,128)S(1)}, s32[256,8]{0,1:T(8,128)}, u32[]{:S(2)}) copy-start(s32[256,8]{0,1:T(8,128)} %param.15) | copy-start | bytes 24580
  40.3 7.3 %copy-start.11 = (bf16[64,512]{1,0:T(8,128)(2,1)S(1)}, bf16[64,512]{1,0:T(8,128)(2,1)}, u32[]{:S(2)}) copy-start(bf16[64,512]{1,0:T(8,128)(2,1)} %param.14) | copy-start | bytes 196612
  61.8 81.7 %copy-start.10 = (bf16[256,512]{1,0:T(8,128)(2,1)}, bf16[256,512]{1,0:T(8,128)(2,1)S(1)}, u32[]{:S(2)}) copy-start(bf16[256,512]{1,0:T(8,128)(2,1)S(1)} %all_gather.3) | copy-start | bytes 786436
  70.5 42.3 %all-to-all-start.2 = ((bf16[8,4,96,512]{3,2,1,0:T(8,128)(2,1)}), bf16[8,4,96,512]{3,2,1,0:T(8,128)(2,1)}, u32[]{:S(2)}, u32[]{:S(2)}) async-start(bf16[8,4,96,512]{3,2,1,0:T(8,128)(2,1)} %convert_bitcast_fusion.1), calls=%async_computation.2 | async-start | bytes 6291456 | tf_op jit(solution)/shard_map/all_to_all | solution.py:39
  81.8 3.4 %copy-start.3 = (bf16[16,112,512]{2,1,0:T(8,128)(2,1)}, bf16[16,112,512]{2,1,0:T(8,128)(2,1)S(1)}, u32[]{:S(2)}) copy-start(bf16[16,112,512]{2,1,0:T(8,128)(2,1)S(1)} %copy.42) | copy-start | bytes 5505028
  87.5 1.0 copy-start.5
  112.9 25.3 %all-to-all-start.3 = ((bf16[8,4,48,512]{3,2,1,0:T(8,128)(2,1)}), bf16[8,4,48,512]{3,2,1,0:T(8,128)(2,1)}, u32[]{:S(2)}, u32[]{:S(2)}) async-start(bf16[8,4,48,512]{3,2,1,0:T(8,128)(2,1)} %fusion.25), calls=%async_computation.3 | async-start | bytes 3145728 | tf_op jit(solution)/shard_map/all_to_all | solution.py:39
  123.7 3.0 %copy-start.4 = (bf16[16,96,512]{2,1,0:T(8,128)(2,1)}, bf16[16,96,512]{2,1,0:T(8,128)(2,1)S(1)}, u32[]{:S(2)}) copy-start(bf16[16,96,512]{2,1,0:T(8,128)(2,1)S(1)} %copy.45) | copy-start | bytes 4718596
  126.7 2.1 %copy-start.1 = (bf16[1536,512]{1,0:T(8,128)(2,1)}, bf16[1536,512]{1,0:T(8,128)(2,1)S(1)}, u32[]{:S(2)}) copy-start(bf16[1536,512]{1,0:T(8,128)(2,1)S(1)} %get-tuple-element.41) | copy-start | bytes 4718596
  128.9 1.4 copy-start.8
  130.3 8.0 %copy-start.6 = (bf16[16,48,512]{2,1,0:T(8,128)(2,1)S(1)}, bf16[16,48,512]{2,1,0:T(8,128)(2,1)}, u32[]{:S(2)}) copy-start(bf16[16,48,512]{2,1,0:T(8,128)(2,1)} %slice.92) | copy-start | bytes 2359300
  141.6 1.9 copy-start.7
  143.5 1.3 copy-start.2
  144.8 0.8 copy-start.9
  177.4 24.4 %all-to-all-start.5 = ((bf16[32,24,512]{2,1,0:T(8,128)(2,1)}), bf16[32,24,512]{2,1,0:T(8,128)(2,1)}, u32[]{:S(2)}, u32[]{:S(2)}) async-start(bf16[32,24,512]{2,1,0:T(8,128)(2,1)} %broadcast_in_dim.22), calls=%async_computation.5 | async-start | bytes 1572864 | tf_op jit(solution)/shard_map/all_to_all | solution.py:104
